TPU v7x, 32 devices: a whole 2x2x4 slice. The times are simulated.
32 devices in a mesh: dp: 4 (over x, core), ctx: 8 (over z, y).
Axes of the slice: x: 2, y: 2, z: 4, core: 2. Of those that a mesh axis runs over, the one named last changes fastest.
Arguments:
- query: bfloat16 [32, 2, 64, 4096], P(('dp', 'ctx')), may hold values from -8 to 8
- keys: bfloat16 [32, 2, 64, 512], P(('dp', 'ctx')), may hold values from -8 to 8
- values: bfloat16 [32, 2, 64, 512], P(('dp', 'ctx')), may hold values from -6 to 6
- grad_out: bfloat16 [32, 2, 64, 4096], P(('dp', 'ctx')), may hold values from -6 to 6
- lengths: int32 [32], replicated, may hold values from 1 to 192, 4096 in all
Outputs:
- grad_query: bfloat16 [32, 2, 64, 4096], P(('dp', 'ctx'))
- grad_keys: bfloat16 [32, 2, 64, 512], P(('dp', 'ctx'))
- grad_values: bfloat16 [32, 2, 64, 512], P(('dp', 'ctx'))
Inputs may be any that keep to these rules, and one draw needn't show every extreme that they name: lengths sum to 4096, and the largest is 192.
All inputs are finite; a program needn't handle non-finite values.
Results may differ from a plain program's by a relative error of at most 0.025.
Values may be sent and summed in bfloat16 or wider, within the bound.
A program may use at most 64 MiB of HBM per device.

v0:
```python
import math

import jax
import jax.numpy as jnp
from jax import lax
from jax.sharding import PartitionSpec as P

HEAD = 128
REACH = 3


def passed_along(value, axis, steps):
    count = lax.axis_size(axis)
    leading, last = (max(0, -steps), min(count, count - steps))
    return lax.ppermute(value, axis, [(source, source + steps) for source in range(leading, last)])


def doc_index(position, doc_ends):
    return jnp.sum((doc_ends[None, :] <= position[:, None]).astype(jnp.int32), axis=1)


def on_device(query, keys, values, grad_out, lengths):
    shards = lax.axis_size(("dp", "ctx"))
    my_index = lax.axis_index(("dp", "ctx"))
    half_rows = query.shape[2]
    local_rows = 2 * half_rows
    head_size = HEAD
    kv_width = keys.shape[3]
    kv_count = kv_width // head_size
    group_size = query.shape[3] // kv_width
    reach = REACH
    window = (reach + 1) * half_rows
    score_scale = 1.0 / math.sqrt(head_size)
    query_halves = query.reshape(2, half_rows, kv_count, group_size, head_size)
    grad_halves = grad_out.reshape(2, half_rows, kv_count, group_size, head_size)
    own_keys = keys.reshape(2, half_rows, kv_count, head_size)
    own_values = values.reshape(2, half_rows, kv_count, head_size)
    doc_ends = jnp.cumsum(lengths)
    block_ids = jnp.stack([my_index, 2 * shards - 1 - my_index])
    query_pos = block_ids[:, None] * half_rows + jnp.arange(half_rows, dtype=jnp.int32)[None, :]
    query_doc = doc_index(query_pos.reshape(-1), doc_ends).reshape(2, half_rows)
    key_pos = (block_ids[:, None] - reach) * half_rows + jnp.arange(window, dtype=jnp.int32)[
        None, :
    ]
    key_doc = doc_index(key_pos.reshape(-1), doc_ends).reshape(2, window)
    allowed = (
        (key_pos[:, None, :] >= 0)
        & (key_pos[:, None, :] <= query_pos[:, :, None])
        & (key_doc[:, None, :] == query_doc[:, :, None])
    )
    is_turn = my_index == shards - 1
    own = jnp.concatenate(
        [keys.reshape(2, half_rows, kv_width), values.reshape(2, half_rows, kv_width)], 2
    )

    def move_up(pair):
        early_in = passed_along(pair[0], ("dp", "ctx"), 1)
        late_in = passed_along(pair[1], ("dp", "ctx"), -1)
        late_in = jnp.where(is_turn, pair[0], late_in)
        return jnp.stack([early_in, late_in])

    def climb(step, carried):
        current, stacked = carried
        current = move_up(current)
        stacked = lax.dynamic_update_index_in_dim(stacked, current, reach - step, 1)
        return (current, stacked)

    windows = jnp.zeros((2, reach + 1, half_rows, 2 * kv_width), jnp.bfloat16)
    windows = windows.at[:, reach].set(own)
    moved, windows = lax.fori_loop(1, reach + 1, climb, (own, windows))
    query_grads = []
    log_totals = []
    deltas = []
    for half_idx in range(2):
        both_win = windows[half_idx].reshape(window, 2 * kv_width)
        key_win = both_win[:, :kv_width].reshape(window, kv_count, head_size)
        value_win = both_win[:, kv_width:].reshape(window, kv_count, head_size)
        visible = allowed[half_idx][None, None]
        scores = (
            jnp.einsum(
                "qghd,kgd->ghqk",
                query_halves[half_idx],
                key_win,
                preferred_element_type=jnp.float32,
            )
            * score_scale
        )
        masked = jnp.where(visible, scores, -1e30)
        row_top = jnp.max(masked, axis=3)
        summed = jnp.sum(jnp.where(visible, jnp.exp(masked - row_top[..., None]), 0.0), axis=3)
        log_total = row_top + jnp.log(summed)
        probs = jnp.where(visible, jnp.exp(scores - log_total[..., None]), 0.0).astype(jnp.bfloat16)
        attn = jnp.einsum(
            "ghqk,kgd->qghd", probs, value_win, preferred_element_type=jnp.float32
        ).astype(jnp.bfloat16)
        delta = jnp.transpose(
            jnp.sum(grad_halves[half_idx].astype(jnp.float32) * attn.astype(jnp.float32), axis=3),
            (1, 2, 0),
        )
        dprob = jnp.einsum(
            "qghd,kgd->ghqk", grad_halves[half_idx], value_win, preferred_element_type=jnp.float32
        )
        dscore = (probs.astype(jnp.float32) * (dprob - delta[..., None]) * score_scale).astype(
            jnp.bfloat16
        )
        query_grads.append(
            jnp.einsum("ghqk,kgd->qghd", dscore, key_win, preferred_element_type=jnp.float32)
        )
        log_totals.append(log_total)
        deltas.append(delta)

    def key_terms(half_idx, pack, step):
        block_query = pack[0][half_idx].astype(jnp.bfloat16)
        block_grad = pack[1][half_idx].astype(jnp.bfloat16)
        far_pos = (block_ids[half_idx] + step) * half_rows + jnp.arange(half_rows, dtype=jnp.int32)
        far_doc = doc_index(far_pos, doc_ends)
        visible = (
            (query_pos[half_idx][None, :] <= far_pos[:, None])
            & (query_doc[half_idx][None, :] == far_doc[:, None])
        )[None, None]
        scores = (
            jnp.einsum(
                "qghd,kgd->ghqk",
                block_query,
                own_keys[half_idx],
                preferred_element_type=jnp.float32,
            )
            * score_scale
        )
        probs = jnp.where(visible, jnp.exp(scores - pack[2][half_idx][..., None]), 0.0).astype(
            jnp.bfloat16
        )
        dprob = jnp.einsum(
            "qghd,kgd->ghqk", block_grad, own_values[half_idx], preferred_element_type=jnp.float32
        )
        dscore = (
            probs.astype(jnp.float32) * (dprob - pack[3][half_idx][..., None]) * score_scale
        ).astype(jnp.bfloat16)
        key_part = jnp.einsum(
            "ghqk,qghd->kgd", dscore, block_query, preferred_element_type=jnp.float32
        ).reshape(half_rows, kv_width)
        value_part = jnp.einsum(
            "ghqk,qghd->kgd", probs, block_grad, preferred_element_type=jnp.float32
        ).reshape(half_rows, kv_width)
        return jnp.concatenate([key_part, value_part], 1)

    def move_query(pack):
        early_in = passed_along((pack[0][0], pack[1][0], pack[2][0], pack[3][0]), ("dp", "ctx"), -1)
        late_in = passed_along((pack[0][1], pack[1][1], pack[2][1], pack[3][1]), ("dp", "ctx"), 1)
        return tuple(
            (
                jnp.stack([jnp.where(is_turn, pack[member][1], early_in[member]), late_in[member]])
                for member in range(4)
            )
        )

    start_pack = (
        query_halves.astype(jnp.float32),
        grad_halves.astype(jnp.float32),
        jnp.stack(log_totals),
        jnp.stack(deltas),
    )
    start_sum = jnp.stack([key_terms(0, start_pack, 0), key_terms(1, start_pack, 0)])

    def sink(step, carried):
        pack, running = carried
        pack = move_query(pack)
        running = running + jnp.stack([key_terms(0, pack, step), key_terms(1, pack, step)])
        return (pack, running)

    final_pack, summed_grads = lax.fori_loop(1, reach + 1, sink, (start_pack, start_sum))
    summed_grads = summed_grads.reshape(local_rows, 2 * kv_width)
    grad_keys = summed_grads[:, :kv_width].astype(jnp.bfloat16).reshape(keys.shape)
    grad_values = summed_grads[:, kv_width:].astype(jnp.bfloat16).reshape(values.shape)
    grad_query = jnp.stack(query_grads).astype(jnp.bfloat16).reshape(query.shape)
    return (grad_query, grad_keys, grad_values)


def solution(mesh):
    in_specs = (
        P(("dp", "ctx"), None, None, None),
        P(("dp", "ctx"), None, None, None),
        P(("dp", "ctx"), None, None, None),
        P(("dp", "ctx"), None, None, None),
        P(),
    )
    out_specs = (
        P(("dp", "ctx"), None, None, None),
        P(("dp", "ctx"), None, None, None),
        P(("dp", "ctx"), None, None, None),
    )
    return jax.shard_map(
        on_device, mesh=mesh, in_specs=in_specs, out_specs=out_specs, check_vma=False
    )
```

profile of v0, /device:TPU:6, one launch (start us, length us, event | category | flops | bytes accessed | tf_op | source)
XLA Modules:
  0.0 351.6 jit_solution(11801181003425426283)
XLA Ops:
  11.1 39.0 %while.39 = (s32[]{:T(128)}, bf16[2,64,1024]{2,1,0:T(8,128)(2,1)S(1)}, bf16[2,4,64,1024]{3,2,0,1:T(8,128)(2,1)S(1)}, pred[]{:T(512)}, s32[]{:T(128)}, /*index=5*/s32[]{:T(128)}, s32[]{:T(128)}, s32[]{:T(128)}) while((s32[]{:T(128)}, bf16[2,64,1024]{2,1,0:T(8,128)(2,1)S(1)}, bf16[2,4,64,1024]{3,2,0,1:T(8,128)(2,1)S(1)}, pred[]{:T(512)}, ...), condition=%wide.region_1.2_spmd, body=%wide.region_0.0_spmd.sunk | while | flops 589830 | bytes 2752728 | solution.py:70
  19.2 4.6 %collective-permute-done.1 = bf16[64,1024]{1,0:T(8,128)(2,1)S(1)} collective-permute-done((bf16[64,1024]{1,0:T(8,128)(2,1)S(1)}, bf16[64,1024]{1,0:T(8,128)(2,1)S(1)}, u32[]{:S(2)}, u32[]{:S(2)}) %collective-permute-start.1) | collective-permute-done | bytes 131104 | tf_op jit(solution)/shard_map/while/body/eval_jaxpr/ppermute | solution.py:15
  23.9 6.9 %collective-permute-start = (bf16[64,1024]{1,0:T(8,128)(2,1)S(1)}, bf16[64,1024]{1,0:T(8,128)(2,1)S(1)}, u32[]{:S(2)}, u32[]{:S(2)}) collective-permute-start(bf16[64,1024]{1,0:T(8,128)(2,1)S(1)} %get-tuple-element.644), channel_id=1, source_target_pairs={{1,0},{2,1},{3,2},{4,3},{5,4},{6,5},{7,6},{8,7},{9,8},{10,9},{11,1... | collective-permute-start | bytes 393224 | tf_op jit(solution)/shard_map/while/body/eval_jaxpr/ppermute | solution.py:15
  33.3 4.3 %collective-permute-done.1 = bf16[64,1024]{1,0:T(8,128)(2,1)S(1)} collective-permute-done((bf16[64,1024]{1,0:T(8,128)(2,1)S(1)}, bf16[64,1024]{1,0:T(8,128)(2,1)S(1)}, u32[]{:S(2)}, u32[]{:S(2)}) %collective-permute-start.1) | collective-permute-done | bytes 131104 | tf_op jit(solution)/shard_map/while/body/eval_jaxpr/ppermute | solution.py:15
  37.8 5.4 %collective-permute-start = (bf16[64,1024]{1,0:T(8,128)(2,1)S(1)}, bf16[64,1024]{1,0:T(8,128)(2,1)S(1)}, u32[]{:S(2)}, u32[]{:S(2)}) collective-permute-start(bf16[64,1024]{1,0:T(8,128)(2,1)S(1)} %get-tuple-element.644), channel_id=1, source_target_pairs={{1,0},{2,1},{3,2},{4,3},{5,4},{6,5},{7,6},{8,7},{9,8},{10,9},{11,1... | collective-permute-start | bytes 393224 | tf_op jit(solution)/shard_map/while/body/eval_jaxpr/ppermute | solution.py:15
  45.7 4.3 %collective-permute-done.1 = bf16[64,1024]{1,0:T(8,128)(2,1)S(1)} collective-permute-done((bf16[64,1024]{1,0:T(8,128)(2,1)S(1)}, bf16[64,1024]{1,0:T(8,128)(2,1)S(1)}, u32[]{:S(2)}, u32[]{:S(2)}) %collective-permute-start.1) | collective-permute-done | bytes 131104 | tf_op jit(solution)/shard_map/while/body/eval_jaxpr/ppermute | solution.py:15
  91.6 258.2 %while.40 = (s32[]{:T(128)}, bf16[2,64,4,8,128]{4,1,3,2,0:T(8,128)(2,1)S(1)}, bf16[2,64,4,8,128]{4,1,3,2,0:T(8,128)(2,1)S(1)}, f32[2,4,8,64]{3,2,1,0:T(8,128)S(1...) while((s32[]{:T(128)}, ...), condition=%wide.region_16.17_spmd, body=%wide.region_13.16_spmd.sunk | while | flops 272809984 | bytes 48294884 | solution.py:171
  101.2 6.7 %collective-permute-start.7 = (f32[4,8,64]{2,1,0:T(8,128)S(1)}, f32[4,8,64]{2,1,0:T(8,128)S(1)}, u32[]{:S(2)}, u32[]{:S(2)}) collective-permute-start(f32[4,8,64]{2,1,0:T(8,128)S(1)} %get-tuple-element.669), channel_id=1, source_target_pairs={{1,0},{2,1},{3,2},{4,3},{5,4},{6,5},{7,6},{8,7},{9,8},{10,9},{11,1... | collective-permute-start | bytes 24584 | tf_op jit(solution)/shard_map/while/body/eval_jaxpr/ppermute | solution.py:15
  112.3 7.2 %collective-permute-start.5 = (bf16[64,4,8,128]{3,0,2,1:T(8,128)(2,1)}, bf16[64,4,8,128]{3,0,2,1:T(8,128)(2,1)}, u32[]{:S(2)}, u32[]{:S(2)}) collective-permute-start(bf16[64,4,8,128]{3,0,2,1:T(8,128)(2,1)} %get-tuple-element.666), channel_id=1, source_target_pairs={{1,0},{2,1},{3,2},{4,3},{5,4},{6,5},{7,6},{8,7},{9,8},{10,9},{11,1... | collective-permute-start | bytes 1572872 | tf_op jit(solution)/shard_map/while/body/eval_jaxpr/ppermute | solution.py:15
  119.5 7.2 %collective-permute-start.3 = (bf16[64,4,8,128]{3,0,2,1:T(8,128)(2,1)}, bf16[64,4,8,128]{3,0,2,1:T(8,128)(2,1)}, u32[]{:S(2)}, u32[]{:S(2)}) collective-permute-start(bf16[64,4,8,128]{3,0,2,1:T(8,128)(2,1)} %get-tuple-element.663), channel_id=1, source_target_pairs={{1,0},{2,1},{3,2},{4,3},{5,4},{6,5},{7,6},{8,7},{9,8},{10,9},{11,1... | collective-permute-start | bytes 1572872 | tf_op jit(solution)/shard_map/while/body/eval_jaxpr/ppermute | solution.py:15
  131.7 17.2 %collective-permute-done.5 = bf16[64,4,8,128]{3,0,2,1:T(8,128)(2,1)} collective-permute-done((bf16[64,4,8,128]{3,0,2,1:T(8,128)(2,1)}, bf16[64,4,8,128]{3,0,2,1:T(8,128)(2,1)}, u32[]{:S(2)}, u32[]{:S(2)}) %collective-permute-start.5) | collective-permute-done | bytes 524320 | tf_op jit(solution)/shard_map/while/body/eval_jaxpr/ppermute | solution.py:15
  150.9 8.8 %collective-permute-done.3 = bf16[64,4,8,128]{3,0,2,1:T(8,128)(2,1)} collective-permute-done((bf16[64,4,8,128]{3,0,2,1:T(8,128)(2,1)}, bf16[64,4,8,128]{3,0,2,1:T(8,128)(2,1)}, u32[]{:S(2)}, u32[]{:S(2)}) %collective-permute-start.3) | collective-permute-done | bytes 524320 | tf_op jit(solution)/shard_map/while/body/eval_jaxpr/ppermute | solution.py:15
  178.0 4.4 %collective-permute-start.9 = (f32[4,8,64]{2,1,0:T(8,128)S(1)}, f32[4,8,64]{2,1,0:T(8,128)S(1)}, u32[]{:S(2)}, u32[]{:S(2)}) collective-permute-start(f32[4,8,64]{2,1,0:T(8,128)S(1)} %get-tuple-element.671), channel_id=1, source_target_pairs={{1,0},{2,1},{3,2},{4,3},{5,4},{6,5},{7,6},{8,7},{9,8},{10,9},{11,1... | collective-permute-start | bytes 24584 | tf_op jit(solution)/shard_map/while/body/eval_jaxpr/ppermute | solution.py:15
  184.8 6.8 %collective-permute-start.7 = (f32[4,8,64]{2,1,0:T(8,128)S(1)}, f32[4,8,64]{2,1,0:T(8,128)S(1)}, u32[]{:S(2)}, u32[]{:S(2)}) collective-permute-start(f32[4,8,64]{2,1,0:T(8,128)S(1)} %get-tuple-element.669), channel_id=1, source_target_pairs={{1,0},{2,1},{3,2},{4,3},{5,4},{6,5},{7,6},{8,7},{9,8},{10,9},{11,1... | collective-permute-start | bytes 24584 | tf_op jit(solution)/shard_map/while/body/eval_jaxpr/ppermute | solution.py:15
  196.0 7.2 %collective-permute-start.5 = (bf16[64,4,8,128]{3,0,2,1:T(8,128)(2,1)}, bf16[64,4,8,128]{3,0,2,1:T(8,128)(2,1)}, u32[]{:S(2)}, u32[]{:S(2)}) collective-permute-start(bf16[64,4,8,128]{3,0,2,1:T(8,128)(2,1)} %get-tuple-element.666), channel_id=1, source_target_pairs={{1,0},{2,1},{3,2},{4,3},{5,4},{6,5},{7,6},{8,7},{9,8},{10,9},{11,1... | collective-permute-start | bytes 1572872 | tf_op jit(solution)/shard_map/while/body/eval_jaxpr/ppermute | solution.py:15
  203.3 7.2 %collective-permute-start.3 = (bf16[64,4,8,128]{3,0,2,1:T(8,128)(2,1)}, bf16[64,4,8,128]{3,0,2,1:T(8,128)(2,1)}, u32[]{:S(2)}, u32[]{:S(2)}) collective-permute-start(bf16[64,4,8,128]{3,0,2,1:T(8,128)(2,1)} %get-tuple-element.663), channel_id=1, source_target_pairs={{1,0},{2,1},{3,2},{4,3},{5,4},{6,5},{7,6},{8,7},{9,8},{10,9},{11,1... | collective-permute-start | bytes 1572872 | tf_op jit(solution)/shard_map/while/body/eval_jaxpr/ppermute | solution.py:15
  215.4 19.8 %collective-permute-done.5 = bf16[64,4,8,128]{3,0,2,1:T(8,128)(2,1)} collective-permute-done((bf16[64,4,8,128]{3,0,2,1:T(8,128)(2,1)}, bf16[64,4,8,128]{3,0,2,1:T(8,128)(2,1)}, u32[]{:S(2)}, u32[]{:S(2)}) %collective-permute-start.5) | collective-permute-done | bytes 524320 | tf_op jit(solution)/shard_map/while/body/eval_jaxpr/ppermute | solution.py:15
  237.1 9.2 %collective-permute-done.3 = bf16[64,4,8,128]{3,0,2,1:T(8,128)(2,1)} collective-permute-done((bf16[64,4,8,128]{3,0,2,1:T(8,128)(2,1)}, bf16[64,4,8,128]{3,0,2,1:T(8,128)(2,1)}, u32[]{:S(2)}, u32[]{:S(2)}) %collective-permute-start.3) | collective-permute-done | bytes 524320 | tf_op jit(solution)/shard_map/while/body/eval_jaxpr/ppermute | solution.py:15
  264.7 4.4 %collective-permute-start.9 = (f32[4,8,64]{2,1,0:T(8,128)S(1)}, f32[4,8,64]{2,1,0:T(8,128)S(1)}, u32[]{:S(2)}, u32[]{:S(2)}) collective-permute-start(f32[4,8,64]{2,1,0:T(8,128)S(1)} %get-tuple-element.671), channel_id=1, source_target_pairs={{1,0},{2,1},{3,2},{4,3},{5,4},{6,5},{7,6},{8,7},{9,8},{10,9},{11,1... | collective-permute-start | bytes 24584 | tf_op jit(solution)/shard_map/while/body/eval_jaxpr/ppermute | solution.py:15
  271.5 6.8 %collective-permute-start.7 = (f32[4,8,64]{2,1,0:T(8,128)S(1)}, f32[4,8,64]{2,1,0:T(8,128)S(1)}, u32[]{:S(2)}, u32[]{:S(2)}) collective-permute-start(f32[4,8,64]{2,1,0:T(8,128)S(1)} %get-tuple-element.669), channel_id=1, source_target_pairs={{1,0},{2,1},{3,2},{4,3},{5,4},{6,5},{7,6},{8,7},{9,8},{10,9},{11,1... | collective-permute-start | bytes 24584 | tf_op jit(solution)/shard_map/while/body/eval_jaxpr/ppermute | solution.py:15
  282.7 7.2 %collective-permute-start.5 = (bf16[64,4,8,128]{3,0,2,1:T(8,128)(2,1)}, bf16[64,4,8,128]{3,0,2,1:T(8,128)(2,1)}, u32[]{:S(2)}, u32[]{:S(2)}) collective-permute-start(bf16[64,4,8,128]{3,0,2,1:T(8,128)(2,1)} %get-tuple-element.666), channel_id=1, source_target_pairs={{1,0},{2,1},{3,2},{4,3},{5,4},{6,5},{7,6},{8,7},{9,8},{10,9},{11,1... | collective-permute-start | bytes 1572872 | tf_op jit(solution)/shard_map/while/body/eval_jaxpr/ppermute | solution.py:15
  289.9 7.2 %collective-permute-start.3 = (bf16[64,4,8,128]{3,0,2,1:T(8,128)(2,1)}, bf16[64,4,8,128]{3,0,2,1:T(8,128)(2,1)}, u32[]{:S(2)}, u32[]{:S(2)}) collective-permute-start(bf16[64,4,8,128]{3,0,2,1:T(8,128)(2,1)} %get-tuple-element.663), channel_id=1, source_target_pairs={{1,0},{2,1},{3,2},{4,3},{5,4},{6,5},{7,6},{8,7},{9,8},{10,9},{11,1... | collective-permute-start | bytes 1572872 | tf_op jit(solution)/shard_map/while/body/eval_jaxpr/ppermute | solution.py:15
  302.1 20.2 %collective-permute-done.5 = bf16[64,4,8,128]{3,0,2,1:T(8,128)(2,1)} collective-permute-done((bf16[64,4,8,128]{3,0,2,1:T(8,128)(2,1)}, bf16[64,4,8,128]{3,0,2,1:T(8,128)(2,1)}, u32[]{:S(2)}, u32[]{:S(2)}) %collective-permute-start.5) | collective-permute-done | bytes 524320 | tf_op jit(solution)/shard_map/while/body/eval_jaxpr/ppermute | solution.py:15
  324.2 9.2 %collective-permute-done.3 = bf16[64,4,8,128]{3,0,2,1:T(8,128)(2,1)} collective-permute-done((bf16[64,4,8,128]{3,0,2,1:T(8,128)(2,1)}, bf16[64,4,8,128]{3,0,2,1:T(8,128)(2,1)}, u32[]{:S(2)}, u32[]{:S(2)}) %collective-permute-start.3) | collective-permute-done | bytes 524320 | tf_op jit(solution)/shard_map/while/body/eval_jaxpr/ppermute | solution.py:15
  (387 shorter events, 166.4 us)
Async XLA Ops:
  91.6 38.1 %collective-permute-start.8 = (f32[4,8,64]{2,1,0:T(8,128)S(1)}, f32[4,8,64]{2,1,0:T(8,128)S(1)}, u32[]{:S(2)}, u32[]{:S(2)}) collective-permute-start(f32[4,8,64]{2,1,0:T(8,128)S(1)} %get-tuple-element.670), channel_id=1, source_target_pairs={{0,1},{1,2},{2,3},{3,4},{4,5},{5,6},{6,7},{7,8},{8,9},{9,10},{10,1... | collective-permute-start | bytes 24584 | tf_op jit(solution)/shard_map/while/body/eval_jaxpr/ppermute | solution.py:15
  94.4 17.8 %collective-permute-start.9 = (f32[4,8,64]{2,1,0:T(8,128)S(1)}, f32[4,8,64]{2,1,0:T(8,128)S(1)}, u32[]{:S(2)}, u32[]{:S(2)}) collective-permute-start(f32[4,8,64]{2,1,0:T(8,128)S(1)} %get-tuple-element.671), channel_id=1, source_target_pairs={{1,0},{2,1},{3,2},{4,3},{5,4},{6,5},{7,6},{8,7},{9,8},{10,9},{11,1... | collective-permute-start | bytes 24584 | tf_op jit(solution)/shard_map/while/body/eval_jaxpr/ppermute | solution.py:15
  98.7 28.9 %collective-permute-start.6 = (f32[4,8,64]{2,1,0:T(8,128)S(1)}, f32[4,8,64]{2,1,0:T(8,128)S(1)}, u32[]{:S(2)}, u32[]{:S(2)}) collective-permute-start(f32[4,8,64]{2,1,0:T(8,128)S(1)} %get-tuple-element.668), channel_id=1, source_target_pairs={{0,1},{1,2},{2,3},{3,4},{4,5},{5,6},{6,7},{7,8},{8,9},{9,10},{10,1... | collective-permute-start | bytes 24584 | tf_op jit(solution)/shard_map/while/body/eval_jaxpr/ppermute | solution.py:15
  101.2 18.3 %collective-permute-start.7 = (f32[4,8,64]{2,1,0:T(8,128)S(1)}, f32[4,8,64]{2,1,0:T(8,128)S(1)}, u32[]{:S(2)}, u32[]{:S(2)}) collective-permute-start(f32[4,8,64]{2,1,0:T(8,128)S(1)} %get-tuple-element.669), channel_id=1, source_target_pairs={{1,0},{2,1},{3,2},{4,3},{5,4},{6,5},{7,6},{8,7},{9,8},{10,9},{11,1... | collective-permute-start | bytes 24584 | tf_op jit(solution)/shard_map/while/body/eval_jaxpr/ppermute | solution.py:15
  108.9 54.6 %collective-permute-start.4 = (bf16[64,4,8,128]{3,0,2,1:T(8,128)(2,1)}, bf16[64,4,8,128]{3,0,2,1:T(8,128)(2,1)S(1)}, u32[]{:S(2)}, u32[]{:S(2)}) collective-permute-start(bf16[64,4,8,128]{3,0,2,1:T(8,128)(2,1)} %get-tuple-element.665), channel_id=1, source_target_pairs={{0,1},{1,2},{2,3},{3,4},{4,5},{5,6},{6,7},{7,8},{8,9},{9,10},{10,1... | collective-permute-start | bytes 1572872 | tf_op jit(solution)/shard_map/while/body/eval_jaxpr/ppermute | solution.py:15
  112.3 36.7 %collective-permute-start.5 = (bf16[64,4,8,128]{3,0,2,1:T(8,128)(2,1)}, bf16[64,4,8,128]{3,0,2,1:T(8,128)(2,1)}, u32[]{:S(2)}, u32[]{:S(2)}) collective-permute-start(bf16[64,4,8,128]{3,0,2,1:T(8,128)(2,1)} %get-tuple-element.666), channel_id=1, source_target_pairs={{1,0},{2,1},{3,2},{4,3},{5,4},{6,5},{7,6},{8,7},{9,8},{10,9},{11,1... | collective-permute-start | bytes 1572872 | tf_op jit(solution)/shard_map/while/body/eval_jaxpr/ppermute | solution.py:15
  119.5 40.2 %collective-permute-start.3 = (bf16[64,4,8,128]{3,0,2,1:T(8,128)(2,1)}, bf16[64,4,8,128]{3,0,2,1:T(8,128)(2,1)}, u32[]{:S(2)}, u32[]{:S(2)}) collective-permute-start(bf16[64,4,8,128]{3,0,2,1:T(8,128)(2,1)} %get-tuple-element.663), channel_id=1, source_target_pairs={{1,0},{2,1},{3,2},{4,3},{5,4},{6,5},{7,6},{8,7},{9,8},{10,9},{11,1... | collective-permute-start | bytes 1572872 | tf_op jit(solution)/shard_map/while/body/eval_jaxpr/ppermute | solution.py:15
  127.7 40.1 %collective-permute-start.2 = (bf16[64,4,8,128]{3,0,2,1:T(8,128)(2,1)}, bf16[64,4,8,128]{3,0,2,1:T(8,128)(2,1)S(1)}, u32[]{:S(2)}, u32[]{:S(2)}) collective-permute-start(bf16[64,4,8,128]{3,0,2,1:T(8,128)(2,1)} %get-tuple-element.662), channel_id=1, source_target_pairs={{0,1},{1,2},{2,3},{3,4},{4,5},{5,6},{6,7},{7,8},{8,9},{9,10},{10,1... | collective-permute-start | bytes 1572872 | tf_op jit(solution)/shard_map/while/body/eval_jaxpr/ppermute | solution.py:15
  176.1 37.3 %collective-permute-start.8 = (f32[4,8,64]{2,1,0:T(8,128)S(1)}, f32[4,8,64]{2,1,0:T(8,128)S(1)}, u32[]{:S(2)}, u32[]{:S(2)}) collective-permute-start(f32[4,8,64]{2,1,0:T(8,128)S(1)} %get-tuple-element.670), channel_id=1, source_target_pairs={{0,1},{1,2},{2,3},{3,4},{4,5},{5,6},{6,7},{7,8},{8,9},{9,10},{10,1... | collective-permute-start | bytes 24584 | tf_op jit(solution)/shard_map/while/body/eval_jaxpr/ppermute | solution.py:15
  178.0 17.9 %collective-permute-start.9 = (f32[4,8,64]{2,1,0:T(8,128)S(1)}, f32[4,8,64]{2,1,0:T(8,128)S(1)}, u32[]{:S(2)}, u32[]{:S(2)}) collective-permute-start(f32[4,8,64]{2,1,0:T(8,128)S(1)} %get-tuple-element.671), channel_id=1, source_target_pairs={{1,0},{2,1},{3,2},{4,3},{5,4},{6,5},{7,6},{8,7},{9,8},{10,9},{11,1... | collective-permute-start | bytes 24584 | tf_op jit(solution)/shard_map/while/body/eval_jaxpr/ppermute | solution.py:15
  182.4 28.9 %collective-permute-start.6 = (f32[4,8,64]{2,1,0:T(8,128)S(1)}, f32[4,8,64]{2,1,0:T(8,128)S(1)}, u32[]{:S(2)}, u32[]{:S(2)}) collective-permute-start(f32[4,8,64]{2,1,0:T(8,128)S(1)} %get-tuple-element.668), channel_id=1, source_target_pairs={{0,1},{1,2},{2,3},{3,4},{4,5},{5,6},{6,7},{7,8},{8,9},{9,10},{10,1... | collective-permute-start | bytes 24584 | tf_op jit(solution)/shard_map/while/body/eval_jaxpr/ppermute | solution.py:15
  184.8 18.4 %collective-permute-start.7 = (f32[4,8,64]{2,1,0:T(8,128)S(1)}, f32[4,8,64]{2,1,0:T(8,128)S(1)}, u32[]{:S(2)}, u32[]{:S(2)}) collective-permute-start(f32[4,8,64]{2,1,0:T(8,128)S(1)} %get-tuple-element.669), channel_id=1, source_target_pairs={{1,0},{2,1},{3,2},{4,3},{5,4},{6,5},{7,6},{8,7},{9,8},{10,9},{11,1... | collective-permute-start | bytes 24584 | tf_op jit(solution)/shard_map/while/body/eval_jaxpr/ppermute | solution.py:15
  192.7 57.6 %collective-permute-start.4 = (bf16[64,4,8,128]{3,0,2,1:T(8,128)(2,1)}, bf16[64,4,8,128]{3,0,2,1:T(8,128)(2,1)S(1)}, u32[]{:S(2)}, u32[]{:S(2)}) collective-permute-start(bf16[64,4,8,128]{3,0,2,1:T(8,128)(2,1)} %get-tuple-element.665), channel_id=1, source_target_pairs={{0,1},{1,2},{2,3},{3,4},{4,5},{5,6},{6,7},{7,8},{8,9},{9,10},{10,1... | collective-permute-start | bytes 1572872 | tf_op jit(solution)/shard_map/while/body/eval_jaxpr/ppermute | solution.py:15
  196.0 39.2 %collective-permute-start.5 = (bf16[64,4,8,128]{3,0,2,1:T(8,128)(2,1)}, bf16[64,4,8,128]{3,0,2,1:T(8,128)(2,1)}, u32[]{:S(2)}, u32[]{:S(2)}) collective-permute-start(bf16[64,4,8,128]{3,0,2,1:T(8,128)(2,1)} %get-tuple-element.666), channel_id=1, source_target_pairs={{1,0},{2,1},{3,2},{4,3},{5,4},{6,5},{7,6},{8,7},{9,8},{10,9},{11,1... | collective-permute-start | bytes 1572872 | tf_op jit(solution)/shard_map/while/body/eval_jaxpr/ppermute | solution.py:15
  203.3 43.1 %collective-permute-start.3 = (bf16[64,4,8,128]{3,0,2,1:T(8,128)(2,1)}, bf16[64,4,8,128]{3,0,2,1:T(8,128)(2,1)}, u32[]{:S(2)}, u32[]{:S(2)}) collective-permute-start(bf16[64,4,8,128]{3,0,2,1:T(8,128)(2,1)} %get-tuple-element.663), channel_id=1, source_target_pairs={{1,0},{2,1},{3,2},{4,3},{5,4},{6,5},{7,6},{8,7},{9,8},{10,9},{11,1... | collective-permute-start | bytes 1572872 | tf_op jit(solution)/shard_map/while/body/eval_jaxpr/ppermute | solution.py:15
  211.4 43.0 %collective-permute-start.2 = (bf16[64,4,8,128]{3,0,2,1:T(8,128)(2,1)}, bf16[64,4,8,128]{3,0,2,1:T(8,128)(2,1)S(1)}, u32[]{:S(2)}, u32[]{:S(2)}) collective-permute-start(bf16[64,4,8,128]{3,0,2,1:T(8,128)(2,1)} %get-tuple-element.662), channel_id=1, source_target_pairs={{0,1},{1,2},{2,3},{3,4},{4,5},{5,6},{6,7},{7,8},{8,9},{9,10},{10,1... | collective-permute-start | bytes 1572872 | tf_op jit(solution)/shard_map/while/body/eval_jaxpr/ppermute | solution.py:15
  262.8 37.3 %collective-permute-start.8 = (f32[4,8,64]{2,1,0:T(8,128)S(1)}, f32[4,8,64]{2,1,0:T(8,128)S(1)}, u32[]{:S(2)}, u32[]{:S(2)}) collective-permute-start(f32[4,8,64]{2,1,0:T(8,128)S(1)} %get-tuple-element.670), channel_id=1, source_target_pairs={{0,1},{1,2},{2,3},{3,4},{4,5},{5,6},{6,7},{7,8},{8,9},{9,10},{10,1... | collective-permute-start | bytes 24584 | tf_op jit(solution)/shard_map/while/body/eval_jaxpr/ppermute | solution.py:15
  264.7 18.0 %collective-permute-start.9 = (f32[4,8,64]{2,1,0:T(8,128)S(1)}, f32[4,8,64]{2,1,0:T(8,128)S(1)}, u32[]{:S(2)}, u32[]{:S(2)}) collective-permute-start(f32[4,8,64]{2,1,0:T(8,128)S(1)} %get-tuple-element.671), channel_id=1, source_target_pairs={{1,0},{2,1},{3,2},{4,3},{5,4},{6,5},{7,6},{8,7},{9,8},{10,9},{11,1... | collective-permute-start | bytes 24584 | tf_op jit(solution)/shard_map/while/body/eval_jaxpr/ppermute | solution.py:15
  269.1 28.9 %collective-permute-start.6 = (f32[4,8,64]{2,1,0:T(8,128)S(1)}, f32[4,8,64]{2,1,0:T(8,128)S(1)}, u32[]{:S(2)}, u32[]{:S(2)}) collective-permute-start(f32[4,8,64]{2,1,0:T(8,128)S(1)} %get-tuple-element.668), channel_id=1, source_target_pairs={{0,1},{1,2},{2,3},{3,4},{4,5},{5,6},{6,7},{7,8},{8,9},{9,10},{10,1... | collective-permute-start | bytes 24584 | tf_op jit(solution)/shard_map/while/body/eval_jaxpr/ppermute | solution.py:15
  271.5 18.5 %collective-permute-start.7 = (f32[4,8,64]{2,1,0:T(8,128)S(1)}, f32[4,8,64]{2,1,0:T(8,128)S(1)}, u32[]{:S(2)}, u32[]{:S(2)}) collective-permute-start(f32[4,8,64]{2,1,0:T(8,128)S(1)} %get-tuple-element.669), channel_id=1, source_target_pairs={{1,0},{2,1},{3,2},{4,3},{5,4},{6,5},{7,6},{8,7},{9,8},{10,9},{11,1... | collective-permute-start | bytes 24584 | tf_op jit(solution)/shard_map/while/body/eval_jaxpr/ppermute | solution.py:15
  279.4 58.0 %collective-permute-start.4 = (bf16[64,4,8,128]{3,0,2,1:T(8,128)(2,1)}, bf16[64,4,8,128]{3,0,2,1:T(8,128)(2,1)S(1)}, u32[]{:S(2)}, u32[]{:S(2)}) collective-permute-start(bf16[64,4,8,128]{3,0,2,1:T(8,128)(2,1)} %get-tuple-element.665), channel_id=1, source_target_pairs={{0,1},{1,2},{2,3},{3,4},{4,5},{5,6},{6,7},{7,8},{8,9},{9,10},{10,1... | collective-permute-start | bytes 1572872 | tf_op jit(solution)/shard_map/while/body/eval_jaxpr/ppermute | solution.py:15
  282.7 39.6 %collective-permute-start.5 = (bf16[64,4,8,128]{3,0,2,1:T(8,128)(2,1)}, bf16[64,4,8,128]{3,0,2,1:T(8,128)(2,1)}, u32[]{:S(2)}, u32[]{:S(2)}) collective-permute-start(bf16[64,4,8,128]{3,0,2,1:T(8,128)(2,1)} %get-tuple-element.666), channel_id=1, source_target_pairs={{1,0},{2,1},{3,2},{4,3},{5,4},{6,5},{7,6},{8,7},{9,8},{10,9},{11,1... | collective-permute-start | bytes 1572872 | tf_op jit(solution)/shard_map/while/body/eval_jaxpr/ppermute | solution.py:15
  289.9 43.5 %collective-permute-start.3 = (bf16[64,4,8,128]{3,0,2,1:T(8,128)(2,1)}, bf16[64,4,8,128]{3,0,2,1:T(8,128)(2,1)}, u32[]{:S(2)}, u32[]{:S(2)}) collective-permute-start(bf16[64,4,8,128]{3,0,2,1:T(8,128)(2,1)} %get-tuple-element.663), channel_id=1, source_target_pairs={{1,0},{2,1},{3,2},{4,3},{5,4},{6,5},{7,6},{8,7},{9,8},{10,9},{11,1... | collective-permute-start | bytes 1572872 | tf_op jit(solution)/shard_map/while/body/eval_jaxpr/ppermute | solution.py:15
  298.1 43.4 %collective-permute-start.2 = (bf16[64,4,8,128]{3,0,2,1:T(8,128)(2,1)}, bf16[64,4,8,128]{3,0,2,1:T(8,128)(2,1)S(1)}, u32[]{:S(2)}, u32[]{:S(2)}) collective-permute-start(bf16[64,4,8,128]{3,0,2,1:T(8,128)(2,1)} %get-tuple-element.662), channel_id=1, source_target_pairs={{0,1},{1,2},{2,3},{3,4},{4,5},{5,6},{6,7},{7,8},{8,9},{9,10},{10,1... | collective-permute-start | bytes 1572872 | tf_op jit(solution)/shard_map/while/body/eval_jaxpr/ppermute | solution.py:15
  (75 other events, 461.8 us)
where the time goes:
time: 356 us; the launch traced here: 352 us
  starting transfers between devices  125 us (35%)
  waiting for transfers between devices  100 us (28%)
  matrix products  45.4 us (13%)
  local copies, waits for them, and re-layouts  41.9 us (12%)
  other arithmetic  36.5 us (10%)
    ppermute x30, starting transfers between devices, passed_along(): lax.ppermute(value, axis, [(source, source + steps) for source in range(l...  125 us
    ppermute x30, waiting for transfers between devices, passed_along(): lax.ppermute(value, axis, [(source, source + steps) for source in range(l...  100 us
    dot_general x8, matrix products, key_terms(): jnp.einsum('ghqk,qghd->kgd', dscore, block_query, preferred_element_type=...  10.7 us
    dot_general x8, matrix products, key_terms(): jnp.einsum('qghd,kgd->ghqk', block_query, own_keys[half_idx], preferred_e...  10.5 us
    dot_general x8, matrix products, key_terms(): jnp.einsum('ghqk,qghd->kgd', probs, block_grad, preferred_element_type=jn...  8.43 us
  transfers between devices with their start and end apart: 30, of which 12 were waited for; matrix products, arithmetic and copies ran while one was open for 13% of the time, Pallas kernels for 0%

commit v1 on v0

v1 whole, which is shorter than its diff:
```python
import functools
import math

import jax
import jax.numpy as jnp
from jax import lax
from jax.experimental import pallas as pl
from jax.experimental.pallas import tpu as pltpu
from jax.sharding import PartitionSpec as P

HEAD = 128
REACH = 3
LANES = 128
NT = (((1,), (1,)), ((), ()))
NN = (((1,), (0,)), ((), ()))


def kernel(
    shards,
    ctx_count,
    sizes,
    lengths,
    query,
    keys,
    values,
    grad_out,
    grad_query,
    grad_keys,
    grad_values,
    q_buf,
    do_buf,
    dq_buf,
    k_win,
    v_win,
    part_out,
    part_in,
    own_sum,
    bias,
    load_sem,
    own_sem,
    store_sem,
    kv_send,
    kv_recv,
    part_send,
    part_recv,
):
    half_rows, kv_count, group_size, doc_count = sizes
    kv_width = kv_count * HEAD
    wide = group_size * HEAD
    window = (REACH + 1) * half_rows
    scale = 1.0 / math.sqrt(HEAD)
    me = lax.axis_index("dp") * ctx_count + lax.axis_index("ctx")

    def place(index):
        return {"dp": lax.div(index, ctx_count), "ctx": lax.rem(index, ctx_count)}

    loads = []
    for half in range(2):
        loads.append(
            (
                pltpu.make_async_copy(query.at[0, half], q_buf.at[half], load_sem.at[half, 0]),
                pltpu.make_async_copy(grad_out.at[0, half], do_buf.at[half], load_sem.at[half, 1]),
                pltpu.make_async_copy(keys.at[0, half], k_win.at[half, REACH], own_sem.at[half, 0]),
                pltpu.make_async_copy(
                    values.at[0, half], v_win.at[half, REACH], own_sem.at[half, 1]
                ),
            )
        )

    barrier = pltpu.get_barrier_semaphore()
    for d in range(1, REACH + 1):

        @pl.when(me >= d)
        def _():
            pl.semaphore_signal(barrier, inc=1, device_id=place(me - d))

        @pl.when(me + d < shards)
        def _():
            pl.semaphore_signal(barrier, inc=1, device_id=place(me + d))

    for copies in loads:
        for copy in copies:
            copy.start()
    pl.semaphore_wait(barrier, jnp.minimum(me, REACH) + jnp.minimum(shards - 1 - me, REACH))

    def early_target(d):
        stays = me + d < shards
        return (
            jnp.where(stays, me + d, 2 * shards - 1 - me - d),
            jnp.where(stays, 0, 1),
        )

    def kv_copies(half, d, target, target_half):
        slot = REACH - d
        return [
            pltpu.make_async_remote_copy(
                src_ref=src.at[0, half],
                dst_ref=dst.at[target_half, slot],
                send_sem=kv_send.at[half, d - 1, which],
                recv_sem=kv_recv.at[target_half, d - 1, which],
                device_id=place(target),
            )
            for which, (src, dst) in enumerate(((keys, k_win), (values, v_win)))
        ]

    for d in range(1, REACH + 1):
        target, target_half = early_target(d)

        @pl.when(target != me)
        def _():
            for copy in kv_copies(0, d, target, target_half):
                copy.start()

        @pl.when(target == me)
        def _():
            for which, (src, dst) in enumerate(((keys, k_win), (values, v_win))):
                pltpu.make_async_copy(
                    src.at[0, 0], dst.at[1, REACH - d], kv_recv.at[1, d - 1, which]
                ).start()

        @pl.when(me >= d)
        def _():
            for copy in kv_copies(1, d, me - d, 1):
                copy.start()

    for d in range(1, REACH + 1):

        @pl.when(me < d)
        def _():
            k_win[0, REACH - d] = jnp.zeros((half_rows, kv_width), k_win.dtype)
            v_win[0, REACH - d] = jnp.zeros((half_rows, kv_width), v_win.dtype)
            part_in[1, d - 1] = jnp.zeros((half_rows, 2 * kv_width), part_in.dtype)

    lane_row = lax.rem(lax.broadcasted_iota(jnp.int32, (8, LANES), 1), half_rows)
    block_ids = (me, 2 * shards - 1 - me)
    positions = [block * half_rows + lane_row for block in block_ids]

    def doc_step(k, carried):
        end, early, late = carried
        end = end + lengths[k]
        return (
            end,
            jnp.where(positions[0] >= end, end, early),
            jnp.where(positions[1] >= end, end, late),
        )

    zero = jnp.zeros((8, LANES), jnp.int32)
    _, early_start, late_start = lax.fori_loop(0, doc_count, doc_step, (jnp.int32(0), zero, zero))
    for half, start in enumerate((early_start, late_start)):
        key_pos = (block_ids[half] - REACH) * half_rows + lax.broadcasted_iota(
            jnp.int32, (window, LANES), 0
        )
        seen = (key_pos >= start[:1]) & (key_pos <= positions[half][:1])
        bias[half] = jnp.where(seen, 0.0, -1e30)

    def unit(half, g):
        wide_at = pl.ds(pl.multiple_of(g * wide, wide), wide)
        head_at = pl.ds(pl.multiple_of(g * HEAD, HEAD), HEAD)
        value_at = pl.ds(pl.multiple_of(kv_width + g * HEAD, HEAD), HEAD)

        def rows_of(ref):
            block = ref[half, :, wide_at]
            return jnp.concatenate(
                [block[:, h * HEAD : (h + 1) * HEAD] for h in range(group_size)], 0
            )

        q = rows_of(q_buf)
        do = rows_of(do_buf)
        k = k_win[half, :, :, head_at].reshape(window, HEAD)
        v = v_win[half, :, :, head_at].reshape(window, HEAD)
        rows = group_size * half_rows
        hidden = jnp.concatenate([bias[half]] * (rows // LANES), 1)
        scores = lax.dot_general(k, q, NT, preferred_element_type=jnp.float32)
        scores = scores * (scale * math.log2(math.e)) + hidden
        top = jnp.max(scores, axis=0, keepdims=True)
        probs = jnp.exp2(scores - top)
        probs = probs * (1.0 / jnp.sum(probs, axis=0, keepdims=True))
        dprob = lax.dot_general(v, do, NT, preferred_element_type=jnp.float32)
        delta = jnp.sum(probs * dprob, axis=0, keepdims=True)
        dscore = (probs * (dprob - delta)).astype(jnp.bfloat16)
        probs = probs.astype(jnp.bfloat16)
        dv = lax.dot_general(probs, do, NN, preferred_element_type=jnp.float32)
        dk = lax.dot_general(dscore, q, NN, preferred_element_type=jnp.float32) * scale
        dq = lax.dot_general(k.T, dscore, NN, preferred_element_type=jnp.float32) * scale
        dq = dq.T.astype(jnp.bfloat16)
        dq_buf[half, :, wide_at] = jnp.concatenate(
            [dq[h * half_rows : (h + 1) * half_rows] for h in range(group_size)], 1
        )
        far = REACH * half_rows
        for at, term in ((head_at, dk), (value_at, dv)):
            for d in range(1, REACH + 1):
                top_row = (REACH - d) * half_rows
                part_out[half, d - 1, :, at] = term[top_row : top_row + half_rows].astype(
                    jnp.bfloat16
                )
            own_sum[half, :, at] = term[far:]

    def late_target(d):
        stays = me + d < shards
        return (
            jnp.where(stays, me + d, 2 * shards - 1 - me - d),
            jnp.where(stays, 1, 0),
        )

    def part_copy(half, d, target, target_half):
        return pltpu.make_async_remote_copy(
            src_ref=part_out.at[half, d - 1],
            dst_ref=part_in.at[target_half, d - 1],
            send_sem=part_send.at[half, d - 1],
            recv_sem=part_recv.at[target_half, d - 1],
            device_id=place(target),
        )

    stores = []
    for half in range(2):
        for copy in loads[half]:
            copy.wait()
        for d in range(1, REACH + 1):

            def arrived():
                for copy in kv_copies(half, d, me, half):
                    copy.wait_recv()

            if half == 0:
                pl.when(me >= d)(arrived)
            else:
                arrived()

        lax.fori_loop(0, kv_count, lambda g, c: (unit(half, g), c)[1], 0)
        store = pltpu.make_async_copy(dq_buf.at[half], grad_query.at[0, half], store_sem.at[half])
        store.start()
        stores.append(store)
        for d in range(1, REACH + 1):
            if half == 0:

                @pl.when(me >= d)
                def _():
                    part_copy(0, d, me - d, 0).start()

            else:
                target, target_half = late_target(d)

                @pl.when(target != me)
                def _():
                    part_copy(1, d, target, target_half).start()

                @pl.when(target == me)
                def _():
                    pltpu.make_async_copy(
                        part_out.at[1, d - 1], part_in.at[0, d - 1], part_recv.at[0, d - 1]
                    ).start()

    for half in range(2):
        for d in range(1, REACH + 1):

            def landed():
                part_copy(half, d, me, half).wait_recv()

            if half == 1:
                pl.when(me >= d)(landed)
            else:
                landed()
        total = own_sum[half]
        for d in range(REACH):
            total = total + part_in[half, d].astype(jnp.float32)
        total = total.astype(jnp.bfloat16)
        grad_keys[0, half] = total[:, :kv_width]
        grad_values[0, half] = total[:, kv_width:]

    for store in stores:
        store.wait()
    for d in range(1, REACH + 1):
        target, target_half = early_target(d)

        @pl.when(target != me)
        def _():
            for copy in kv_copies(0, d, target, target_half):
                copy.wait_send()
            part_copy(1, d, target, 1 - target_half).wait_send()

        @pl.when(me >= d)
        def _():
            for copy in kv_copies(1, d, me - d, 1):
                copy.wait_send()
            part_copy(0, d, me - d, 0).wait_send()


def on_device(query, keys, values, grad_out, lengths):
    half_rows = query.shape[2]
    kv_width = keys.shape[3]
    kv_count = kv_width // HEAD
    group_size = query.shape[3] // kv_width
    window = (REACH + 1) * half_rows
    sizes = (half_rows, kv_count, group_size, lengths.shape[0])
    shards = lax.axis_size("dp") * lax.axis_size("ctx")
    bf16, f32 = jnp.bfloat16, jnp.float32
    dma = pltpu.SemaphoreType.DMA
    anywhere = pl.BlockSpec(memory_space=pl.ANY)
    vmem = pl.BlockSpec(memory_space=pltpu.VMEM)
    wide_half = (2, half_rows, query.shape[3])
    return pl.pallas_call(
        functools.partial(kernel, shards, lax.axis_size("ctx"), sizes),
        out_shape=(
            jax.ShapeDtypeStruct(query.shape, bf16),
            jax.ShapeDtypeStruct(keys.shape, bf16),
            jax.ShapeDtypeStruct(values.shape, bf16),
        ),
        in_specs=[pl.BlockSpec(memory_space=pltpu.SMEM)] + [anywhere] * 4,
        out_specs=(anywhere, vmem, vmem),
        scratch_shapes=[
            pltpu.VMEM(wide_half, bf16),
            pltpu.VMEM(wide_half, bf16),
            pltpu.VMEM(wide_half, bf16),
            pltpu.VMEM((2, REACH + 1, half_rows, kv_width), bf16),
            pltpu.VMEM((2, REACH + 1, half_rows, kv_width), bf16),
            pltpu.VMEM((2, REACH, half_rows, 2 * kv_width), bf16),
            pltpu.VMEM((2, REACH, half_rows, 2 * kv_width), bf16),
            pltpu.VMEM((2, half_rows, 2 * kv_width), f32),
            pltpu.VMEM((2, window, LANES), f32),
            dma((2, 2)),
            dma((2, 2)),
            dma((2,)),
            dma((2, REACH, 2)),
            dma((2, REACH, 2)),
            dma((2, REACH)),
            dma((2, REACH)),
        ],
        compiler_params=pltpu.CompilerParams(
            collective_id=0, has_side_effects=True, vmem_limit_bytes=40 * 1024 * 1024
        ),
        cost_estimate=pl.CostEstimate(
            flops=20 * half_rows * window * query.shape[3], bytes_accessed=4 << 20, transcendentals=0
        ),
    )(lengths, query, keys, values, grad_out)


def solution(mesh):
    spec = P(("dp", "ctx"), None, None, None)
    return jax.shard_map(
        on_device,
        mesh=mesh,
        in_specs=(spec, spec, spec, spec, P()),
        out_specs=(spec, spec, spec),
        check_vma=False,
    )
```

time: 356 us -> 51 us (0.14)
  the two profiles are of different devices: /device:TPU:6 before, /device:TPU:11 now
where the time goes in v1:
time: 51 us; the launch traced here: 50.8 us
  Pallas kernels  43 us (84%)
  local copies, waits for them, and re-layouts  7.19 us (14%)
  between operations  0.65 us (1%)
    pallas_call x1, Pallas kernels, on_device(): pl.pallas_call(functools.partial(kernel, shards, lax.axis_size('ctx'), si...  43 us
    unnamed x13, local copies, waits for them, and re-layouts  7.19 us

profile of v1, /device:TPU:11, one launch (start us, length us, event | category | flops | bytes accessed | tf_op | source)
XLA Modules:
  0.0 50.8 jit_solution(712835083421036637)
XLA Ops:
  0.6 0.0 copy-start
  0.6 1.2 %copy-done = bf16[1,2,64,4096]{3,2,1,0:T(8,128)(2,1)S(1)} copy-done((bf16[1,2,64,4096]{3,2,1,0:T(8,128)(2,1)S(1)}, bf16[1,2,64,4096]{3,2,1,0:T(8,128)(2,1)}, u32[]{:S(2)}) %copy-start) | copy-done | bytes 1048600
  1.9 0.0 copy-start.1
  1.9 1.2 %copy-done.1 = bf16[1,2,64,4096]{3,2,1,0:T(8,128)(2,1)S(1)} copy-done((bf16[1,2,64,4096]{3,2,1,0:T(8,128)(2,1)S(1)}, bf16[1,2,64,4096]{3,2,1,0:T(8,128)(2,1)}, u32[]{:S(2)}) %copy-start.1) | copy-done | bytes 1048600
  3.1 0.0 copy-start.2
  3.1 0.9 %copy-done.2 = bf16[1,2,64,512]{3,2,1,0:T(8,128)(2,1)S(1)} copy-done((bf16[1,2,64,512]{3,2,1,0:T(8,128)(2,1)S(1)}, bf16[1,2,64,512]{3,2,1,0:T(8,128)(2,1)}, u32[]{:S(2)}) %copy-start.2) | copy-done | bytes 131096
  4.0 0.0 copy-start.3
  4.0 0.9 %copy-done.3 = bf16[1,2,64,512]{3,2,1,0:T(8,128)(2,1)S(1)} copy-done((bf16[1,2,64,512]{3,2,1,0:T(8,128)(2,1)S(1)}, bf16[1,2,64,512]{3,2,1,0:T(8,128)(2,1)}, u32[]{:S(2)}) %copy-start.3) | copy-done | bytes 131096
  4.9 0.0 copy-start.4
  4.9 0.7 %copy-done.4 = s32[32]{0:T(128)S(1)} copy-done((s32[32]{0:T(128)S(1)}, s32[32]{0:T(128)}, u32[]{:S(2)}) %copy-start.4) | copy-done | bytes 152
  5.5 43.0 %shard_map.76 = (bf16[1,2,64,4096]{3,2,1,0:T(8,128)(2,1)S(1)}, bf16[1,2,64,512]{3,2,1,0:T(8,128)(2,1)S(1)}, bf16[1,2,64,512]{3,2,1,0:T(8,128)(2,1)S(1)}) custom-call(s32[32]{0:T(128)S(1)} %copy-done.4, bf16[1,2,64,4096]{3,2,1,0:T(8,128)(2,1)S(1)} %copy-done, bf16[1,2,64,512]{3,2,1,0:T(8,128)(2,1)S(1)} %copy-done.2, bf16[1,2,64,512]{3,2,1,0:T(8,128)(2,1)S(1)} %copy-done.3, ...), custom_call_target="tpu_custom_call" | custom-call | flops 1342177280 | bytes 4194304 | tf_op jit(solution)/shard_map/pallas_call | solution.py:301
  48.5 1.0 %copy.11 = bf16[1,2,64,4096]{3,2,1,0:T(8,128)(2,1)} copy(bf16[1,2,64,4096]{3,2,1,0:T(8,128)(2,1)S(1)} %get-tuple-element.6) | data formatting | bytes 2097152
  49.5 0.7 %copy.12 = bf16[1,2,64,512]{3,2,1,0:T(8,128)(2,1)} copy(bf16[1,2,64,512]{3,2,1,0:T(8,128)(2,1)S(1)} %get-tuple-element.7) | data formatting | bytes 262144
  50.2 0.7 %copy.13 = bf16[1,2,64,512]{3,2,1,0:T(8,128)(2,1)} copy(bf16[1,2,64,512]{3,2,1,0:T(8,128)(2,1)S(1)} %get-tuple-element.8) | data formatting | bytes 262144
Async XLA Ops:
  0.6 1.2 %copy-start = (bf16[1,2,64,4096]{3,2,1,0:T(8,128)(2,1)S(1)}, bf16[1,2,64,4096]{3,2,1,0:T(8,128)(2,1)}, u32[]{:S(2)}) copy-start(bf16[1,2,64,4096]{3,2,1,0:T(8,128)(2,1)} %query.1) | copy-start | bytes 3145732
  1.9 1.2 %copy-start.1 = (bf16[1,2,64,4096]{3,2,1,0:T(8,128)(2,1)S(1)}, bf16[1,2,64,4096]{3,2,1,0:T(8,128)(2,1)}, u32[]{:S(2)}) copy-start(bf16[1,2,64,4096]{3,2,1,0:T(8,128)(2,1)} %grad_out.1) | copy-start | bytes 3145732
  3.1 0.9 %copy-start.2 = (bf16[1,2,64,512]{3,2,1,0:T(8,128)(2,1)S(1)}, bf16[1,2,64,512]{3,2,1,0:T(8,128)(2,1)}, u32[]{:S(2)}) copy-start(bf16[1,2,64,512]{3,2,1,0:T(8,128)(2,1)} %keys.1) | copy-start | bytes 393220
  4.0 0.9 %copy-start.3 = (bf16[1,2,64,512]{3,2,1,0:T(8,128)(2,1)S(1)}, bf16[1,2,64,512]{3,2,1,0:T(8,128)(2,1)}, u32[]{:S(2)}) copy-start(bf16[1,2,64,512]{3,2,1,0:T(8,128)(2,1)} %values.1) | copy-start | bytes 393220
  4.9 0.7 %copy-start.4 = (s32[32]{0:T(128)S(1)}, s32[32]{0:T(128)}, u32[]{:S(2)}) copy-start(s32[32]{0:T(128)} %lengths.1) | copy-start | bytes 388

commit v2 on v1

v2 whole, which is shorter than its diff:
```python
import functools
import math

import jax
import jax.numpy as jnp
from jax import lax
from jax.experimental import pallas as pl
from jax.experimental.pallas import tpu as pltpu
from jax.sharding import PartitionSpec as P

HEAD = 128
REACH = 3
STAGES = 2
LANES = 128
NT = (((1,), (1,)), ((), ()))
NN = (((1,), (0,)), ((), ()))


def kernel(
    shards,
    ctx_count,
    sizes,
    lengths_hbm,
    query,
    keys,
    values,
    grad_out,
    grad_query,
    grad_keys,
    grad_values,
    lengths,
    q_buf,
    do_buf,
    dq_buf,
    k_win,
    v_win,
    part_out,
    part_in,
    own_sum,
    bias,
    length_sem,
    load_sem,
    own_sem,
    store_sem,
    kv_send,
    kv_recv,
    part_send,
    part_recv,
):
    half_rows, kv_count, group_size, doc_count = sizes
    stages = STAGES
    stage_heads = kv_count // stages
    stage_width = stage_heads * HEAD
    kv_width = kv_count * HEAD
    wide = group_size * HEAD
    window = (REACH + 1) * half_rows
    scale = 1.0 / math.sqrt(HEAD)
    me = lax.axis_index("dp") * ctx_count + lax.axis_index("ctx")
    blocks = (me, 2 * shards - 1 - me)

    def place(index):
        return {"dp": lax.div(index, ctx_count), "ctx": lax.rem(index, ctx_count)}

    def owner(block):
        early = block < shards
        return jnp.where(early, block, 2 * shards - 1 - block), jnp.where(early, 0, 1)

    def exists(block):
        return (block >= 0) & (block < 2 * shards)

    length_load = pltpu.make_async_copy(lengths_hbm, lengths, length_sem.at[0])
    loads = []
    for half in range(2):
        for stage in range(stages):
            at = pl.ds(stage * stage_width, stage_width)
            for which, (mine, win) in enumerate(((keys, k_win), (values, v_win))):
                loads.append(
                    pltpu.make_async_copy(
                        mine.at[0, half, :, at],
                        win.at[half, stage, REACH],
                        own_sem.at[half, which, stage],
                    )
                )
        loads += [
            pltpu.make_async_copy(query.at[0, half], q_buf.at[half], load_sem.at[half, 0]),
            pltpu.make_async_copy(grad_out.at[0, half], do_buf.at[half], load_sem.at[half, 1]),
        ]

    barrier = pltpu.get_barrier_semaphore()
    for d in (1, 2):

        @pl.when(me >= d)
        def _():
            pl.semaphore_signal(barrier, inc=1, device_id=place(me - d))

        @pl.when(me + d < shards)
        def _():
            pl.semaphore_signal(barrier, inc=1, device_id=place(me + d))

    length_load.start()
    for copy in loads:
        copy.start()
    pl.semaphore_wait(barrier, jnp.minimum(me, 2) + jnp.minimum(shards - 1 - me, 2))

    def send(present, src, dst, block, send_sem, recv_sem):
        target, target_half = owner(block)

        @pl.when(present & (target != me))
        def _():
            pltpu.make_async_remote_copy(
                src_ref=src,
                dst_ref=dst(target_half),
                send_sem=send_sem,
                recv_sem=recv_sem(target_half),
                device_id=place(target),
            ).start()

        @pl.when(present & (target == me))
        def _():
            pltpu.make_async_copy(src, dst(target_half), recv_sem(target_half)).start()

    def await_send(present, src, dst, block, send_sem, recv_sem):
        target, target_half = owner(block)

        @pl.when(present & (target != me))
        def _():
            pltpu.make_async_remote_copy(
                src_ref=src,
                dst_ref=dst(target_half),
                send_sem=send_sem,
                recv_sem=recv_sem(target_half),
                device_id=place(target),
            ).wait_send()

    def await_recv(present, dst, send_sem, recv_sem):
        @pl.when(present)
        def _():
            pltpu.make_async_remote_copy(
                src_ref=dst,
                dst_ref=dst,
                send_sem=send_sem,
                recv_sem=recv_sem,
                device_id=place(me),
            ).wait_recv()

    def kv_lanes(stage):
        return pl.ds(pl.multiple_of(stage * stage_width, stage_width), stage_width)

    def kv_send_args(half, d, stage):
        at = kv_lanes(stage)
        for which, (mine, win) in enumerate(((keys, k_win), (values, v_win))):
            if d < REACH:
                block, present = blocks[half] + d, exists(blocks[half] + d)
                src = mine.at[0, half, :, at]
            else:
                block = blocks[half] + 1
                present = exists(block) & exists(blocks[half] - 2)
                src = win.at[half, stage, REACH - 2]

            def dst(target_half, win=win):
                return win.at[target_half, stage, REACH - d]

            def recv(target_half, which=which):
                return kv_recv.at[target_half, d - 1, which, stage]

            yield present, src, dst, block, kv_send.at[half, d - 1, which, stage], recv

    def start_kv(half, d, stage):
        for args in kv_send_args(half, d, stage):
            send(*args)

    def finish_kv(half, d, stage):
        for args in kv_send_args(half, d, stage):
            await_send(*args)

    def await_kv(half, d, stage):
        for which, win in enumerate((k_win, v_win)):
            await_recv(
                exists(blocks[half] - d),
                win.at[half, stage, REACH - d],
                kv_send.at[half, d - 1, which, stage],
                kv_recv.at[half, d - 1, which, stage],
            )

    def relay_kv(stage):
        for half in range(2):
            await_kv(half, 2, stage)
            start_kv(half, 3, stage)

    def part_args(half, d, stage):
        return (
            exists(blocks[half] - d),
            part_out.at[half, stage, d - 1],
            lambda target_half: part_in.at[target_half, stage, d - 1],
            blocks[half] - (1 if d == REACH else d),
            part_send.at[half, d - 1, stage],
            lambda target_half: part_recv.at[target_half, d - 1, stage],
        )

    def finish_part(half, d, stage):
        await_send(*part_args(half, d, stage))

    def await_part(half, d, stage):
        if d == REACH:
            present = exists(blocks[half] + 1) & exists(blocks[half] - 2)
        else:
            present = exists(blocks[half] + d)
        await_recv(
            present,
            part_in.at[half, stage, d - 1],
            part_send.at[half, d - 1, stage],
            part_recv.at[half, d - 1, stage],
        )

    def relay_part(stage):
        for half in range(2):
            await_part(half, 3, stage)
            part_out[half, stage, 1] = (
                part_out[half, stage, 1].astype(jnp.float32)
                + part_in[half, stage, 2].astype(jnp.float32)
            ).astype(jnp.bfloat16)
            send(*part_args(half, 2, stage))

    for stage in range(stages):
        for d in (2, 1):
            for half in range(2):
                start_kv(half, d, stage)

    for d in range(1, REACH + 1):

        @pl.when(me < d)
        def _():
            for stage in range(stages):
                k_win[0, stage, REACH - d] = jnp.zeros((half_rows, stage_width), k_win.dtype)
                v_win[0, stage, REACH - d] = jnp.zeros((half_rows, stage_width), v_win.dtype)

    for half, d, missing in ((0, 3, me < 2), (1, 3, me < 1), (1, 2, me < 2), (1, 1, me < 1)):

        @pl.when(missing)
        def _():
            for stage in range(stages):
                part_in[half, stage, d - 1] = jnp.zeros(
                    (half_rows, 2 * stage_width), part_in.dtype
                )

    lane_row = lax.rem(lax.broadcasted_iota(jnp.int32, (8, LANES), 1), half_rows)
    positions = [block * half_rows + lane_row for block in blocks]

    def doc_step(k, carried):
        end, early, late = carried
        end = end + lengths[k]
        return (
            end,
            jnp.where(positions[0] >= end, end, early),
            jnp.where(positions[1] >= end, end, late),
        )

    length_load.wait()
    zero = jnp.zeros((8, LANES), jnp.int32)
    _, early_start, late_start = lax.fori_loop(0, doc_count, doc_step, (jnp.int32(0), zero, zero))
    for half, start in enumerate((early_start, late_start)):
        key_pos = (blocks[half] - REACH) * half_rows + lax.broadcasted_iota(
            jnp.int32, (window, LANES), 0
        )
        seen = (key_pos >= start[:1]) & (key_pos <= positions[half][:1])
        bias[half] = jnp.where(seen, 0.0, -1e30)

    def unit(half, stage, head):
        g = stage * stage_heads + head
        wide_at = pl.ds(pl.multiple_of(g * wide, wide), wide)
        key_at = pl.ds(pl.multiple_of(head * HEAD, HEAD), HEAD)
        value_at = pl.ds(pl.multiple_of(head * HEAD + stage_width, HEAD), HEAD)

        def rows_of(ref):
            block = ref[half, :, wide_at]
            return jnp.concatenate(
                [block[:, h * HEAD : (h + 1) * HEAD] for h in range(group_size)], 0
            )

        q = rows_of(q_buf)
        do = rows_of(do_buf)
        k = k_win[half, stage, :, :, key_at].reshape(window, HEAD)
        v = v_win[half, stage, :, :, key_at].reshape(window, HEAD)
        rows = group_size * half_rows
        hidden = jnp.concatenate([bias[half]] * (rows // LANES), 1)
        scores = lax.dot_general(k, q, NT, preferred_element_type=jnp.float32)
        scores = scores * (scale * math.log2(math.e)) + hidden
        top = jnp.max(scores, axis=0, keepdims=True)
        probs = jnp.exp2(scores - top)
        probs = probs * (1.0 / jnp.sum(probs, axis=0, keepdims=True))
        dprob = lax.dot_general(v, do, NT, preferred_element_type=jnp.float32)
        delta = jnp.sum(probs * dprob, axis=0, keepdims=True)
        dscore = (probs * (dprob - delta)).astype(jnp.bfloat16)
        probs = probs.astype(jnp.bfloat16)
        dv = lax.dot_general(probs, do, NN, preferred_element_type=jnp.float32)
        dk = lax.dot_general(dscore, q, NN, preferred_element_type=jnp.float32) * scale
        dq = lax.dot_general(k.T, dscore, NN, preferred_element_type=jnp.float32) * scale
        dq = dq.T.astype(jnp.bfloat16)
        dq_buf[half, :, wide_at] = jnp.concatenate(
            [dq[h * half_rows : (h + 1) * half_rows] for h in range(group_size)], 1
        )
        far = REACH * half_rows
        for at, term in ((key_at, dk), (value_at, dv)):
            for d in range(1, REACH + 1):
                top_row = (REACH - d) * half_rows
                part_out[half, stage, d - 1, :, at] = term[top_row : top_row + half_rows].astype(
                    jnp.bfloat16
                )
            own_sum[half, stage, :, at] = term[far:]

    relay_kv(0)
    for copy in loads:
        copy.wait()

    def stage_step(stage, carried):
        for half in range(2):
            for d in (1, 3):
                await_kv(half, d, stage)

        def unit_step(u, inner):
            unit(lax.rem(u, 2), stage, lax.div(u, 2))

            @pl.when((u == 0) & (stage + 1 < stages))
            def _():
                relay_kv(stage + 1)

            @pl.when((u == 1) & (stage > 0))
            def _():
                relay_part(stage - 1)

            return inner

        lax.fori_loop(0, 2 * stage_heads, unit_step, 0)
        for d in (3, 1):
            for half in range(2):
                send(*part_args(half, d, stage))
        return carried

    lax.fori_loop(0, stages, stage_step, 0)
    stores = []
    for half in range(2):
        store = pltpu.make_async_copy(dq_buf.at[half], grad_query.at[0, half], store_sem.at[half])
        store.start()
        stores.append(store)
    relay_part(stages - 1)
    for stage in range(stages):
        for half in range(2):
            for d in (1, 2):
                await_part(half, d, stage)
            total = own_sum[half, stage]
            for d in (1, 2):
                total = total + part_in[half, stage, d - 1].astype(jnp.float32)
            total = total.astype(jnp.bfloat16)
            grad_keys[0, half, :, kv_lanes(stage)] = total[:, :stage_width]
            grad_values[0, half, :, kv_lanes(stage)] = total[:, stage_width:]

    for store in stores:
        store.wait()
    for stage in range(stages):
        for half in range(2):
            for d in range(1, REACH + 1):
                finish_kv(half, d, stage)
                finish_part(half, d, stage)


def on_device(query, keys, values, grad_out, lengths):
    half_rows = query.shape[2]
    kv_width = keys.shape[3]
    kv_count = kv_width // HEAD
    group_size = query.shape[3] // kv_width
    window = (REACH + 1) * half_rows
    sizes = (half_rows, kv_count, group_size, lengths.shape[0])
    shards = lax.axis_size("dp") * lax.axis_size("ctx")
    bf16, f32 = jnp.bfloat16, jnp.float32
    dma = pltpu.SemaphoreType.DMA
    anywhere = pl.BlockSpec(memory_space=pl.ANY)
    in_hbm = pl.BlockSpec(memory_space=pltpu.HBM)
    vmem = pl.BlockSpec(memory_space=pltpu.VMEM)
    wide_half = (2, half_rows, query.shape[3])
    return pl.pallas_call(
        functools.partial(kernel, shards, lax.axis_size("ctx"), sizes),
        out_shape=(
            jax.ShapeDtypeStruct(query.shape, bf16),
            jax.ShapeDtypeStruct(keys.shape, bf16),
            jax.ShapeDtypeStruct(values.shape, bf16),
        ),
        in_specs=[in_hbm] * 5,
        out_specs=(anywhere, vmem, vmem),
        scratch_shapes=[
            pltpu.SMEM(lengths.shape, jnp.int32),
            pltpu.VMEM(wide_half, bf16),
            pltpu.VMEM(wide_half, bf16),
            pltpu.VMEM(wide_half, bf16),
            pltpu.VMEM((2, STAGES, REACH + 1, half_rows, kv_width // STAGES), bf16),
            pltpu.VMEM((2, STAGES, REACH + 1, half_rows, kv_width // STAGES), bf16),
            pltpu.VMEM((2, STAGES, REACH, half_rows, 2 * kv_width // STAGES), bf16),
            pltpu.VMEM((2, STAGES, REACH, half_rows, 2 * kv_width // STAGES), bf16),
            pltpu.VMEM((2, STAGES, half_rows, 2 * kv_width // STAGES), f32),
            pltpu.VMEM((2, window, LANES), f32),
            dma((1,)),
            dma((2, 2)),
            dma((2, 2, STAGES)),
            dma((2,)),
            dma((2, REACH, 2, STAGES)),
            dma((2, REACH, 2, STAGES)),
            dma((2, REACH, STAGES)),
            dma((2, REACH, STAGES)),
        ],
        compiler_params=pltpu.CompilerParams(
            collective_id=0, has_side_effects=True, vmem_limit_bytes=60 * 1024 * 1024
        ),
        cost_estimate=pl.CostEstimate(
            flops=20 * half_rows * window * query.shape[3], bytes_accessed=4 << 20, transcendentals=0
        ),
    )(lengths, query, keys, values, grad_out)


def solution(mesh):
    spec = P(("dp", "ctx"), None, None, None)
    return jax.shard_map(
        on_device,
        mesh=mesh,
        in_specs=(spec, spec, spec, spec, P()),
        out_specs=(spec, spec, spec),
        check_vma=False,
    )
```

time: 51 us -> 45.3 us (0.89)
  the two profiles are of different devices: /device:TPU:11 before, /device:TPU:1 now
where the time goes in v2:
time: 45.3 us; the launch traced here: 45.1 us
  Pallas kernels  40.5 us (89%)
  local copies, waits for them, and re-layouts  3.93 us (9%)
  between operations  0.65 us (1%)
    pallas_call x1, Pallas kernels, on_device(): pl.pallas_call(functools.partial(kernel, shards, lax.axis_size('ctx'), si...  40.5 us
    unnamed x7, local copies, waits for them, and re-layouts  3.93 us

profile of v2, /device:TPU:1, one launch (start us, length us, event | category | flops | bytes accessed | tf_op | source)
XLA Modules:
  0.0 45.1 jit_solution(15222077747362127731)
XLA Ops:
  0.6 40.5 %shard_map.76 = (bf16[1,2,64,4096]{3,2,1,0:T(8,128)(2,1)}, bf16[1,2,64,512]{3,2,1,0:T(8,128)(2,1)}, bf16[1,2,64,512]{3,2,1,0:T(8,128)(2,1)}) custom-call(s32[32]{0:T(128)} %lengths_hbm.1, bf16[1,2,64,4096]{3,2,1,0:T(8,128)(2,1)} %query.1, bf16[1,2,64,512]{3,2,1,0:T(8,128)(2,1)} %keys.1, bf16[1,2,64,512]{3,2,1,0:T(8,128)(2,1)} %values.1, ...), custom_call_target="tpu_custom_call" | custom-call | flops 1342177280 | bytes 4194304 | tf_op jit(solution)/shard_map/pallas_call | solution.py:380
  41.2 0.0 copy-start.1
  41.2 2.3 %copy.11 = bf16[1,2,64,4096]{3,2,1,0:T(8,128)(2,1)} copy(bf16[1,2,64,4096]{3,2,1,0:T(8,128)(2,1)} %get-tuple-element.6) | data formatting | bytes 2097152
  43.5 0.0 copy-done.1
  43.5 0.0 copy-start
  43.5 0.7 %copy.12 = bf16[1,2,64,512]{3,2,1,0:T(8,128)(2,1)} copy(bf16[1,2,64,512]{3,2,1,0:T(8,128)(2,1)S(1)} %copy-done.1) | data formatting | bytes 262144
  44.1 0.3 copy-done
  44.4 0.7 %copy.13 = bf16[1,2,64,512]{3,2,1,0:T(8,128)(2,1)} copy(bf16[1,2,64,512]{3,2,1,0:T(8,128)(2,1)S(1)} %copy-done) | data formatting | bytes 262144
Async XLA Ops:
  41.2 2.3 %copy-start.1 = (bf16[1,2,64,512]{3,2,1,0:T(8,128)(2,1)S(1)}, bf16[1,2,64,512]{3,2,1,0:T(8,128)(2,1)}, u32[]{:S(2)}) copy-start(bf16[1,2,64,512]{3,2,1,0:T(8,128)(2,1)} %get-tuple-element.7) | copy-start | bytes 393220
  43.5 1.0 %copy-start = (bf16[1,2,64,512]{3,2,1,0:T(8,128)(2,1)S(1)}, bf16[1,2,64,512]{3,2,1,0:T(8,128)(2,1)}, u32[]{:S(2)}) copy-start(bf16[1,2,64,512]{3,2,1,0:T(8,128)(2,1)} %get-tuple-element.8) | copy-start | bytes 393220

commit v3 on v2

--- a/solution.py
+++ b/solution.py
@@ -10,7 +10,7 @@
 
 HEAD = 128
 REACH = 3
-STAGES = 2
+STAGES = 4
 LANES = 128
 NT = (((1,), (1,)), ((), ()))
 NN = (((1,), (0,)), ((), ()))

time: 45.3 us -> 51.3 us (1.13)
  the two profiles are of different devices: /device:TPU:1 before, /device:TPU:6 now
where the time goes in v3:
time: 51.3 us; the launch traced here: 51.1 us
  Pallas kernels  46.6 us (91%)
  local copies, waits for them, and re-layouts  3.93 us (8%)
  between operations  0.65 us (1%)
    pallas_call x1, Pallas kernels, on_device(): pl.pallas_call(functools.partial(kernel, shards, lax.axis_size('ctx'), si...  46.6 us
    unnamed x7, local copies, waits for them, and re-layouts  3.93 us

profile of v3, /device:TPU:6, one launch (start us, length us, event | category | flops | bytes accessed | tf_op | source)
XLA Modules:
  0.0 51.1 jit_solution(12509926582986094607)
XLA Ops:
  0.6 46.6 %shard_map.76 = (bf16[1,2,64,4096]{3,2,1,0:T(8,128)(2,1)}, bf16[1,2,64,512]{3,2,1,0:T(8,128)(2,1)}, bf16[1,2,64,512]{3,2,1,0:T(8,128)(2,1)}) custom-call(s32[32]{0:T(128)} %lengths_hbm.1, bf16[1,2,64,4096]{3,2,1,0:T(8,128)(2,1)} %query.1, bf16[1,2,64,512]{3,2,1,0:T(8,128)(2,1)} %keys.1, bf16[1,2,64,512]{3,2,1,0:T(8,128)(2,1)} %values.1, ...), custom_call_target="tpu_custom_call" | custom-call | flops 1342177280 | bytes 4194304 | tf_op jit(solution)/shard_map/pallas_call | solution.py:380
  47.2 0.0 copy-start.1
  47.2 2.3 %copy.11 = bf16[1,2,64,4096]{3,2,1,0:T(8,128)(2,1)} copy(bf16[1,2,64,4096]{3,2,1,0:T(8,128)(2,1)} %get-tuple-element.6) | data formatting | bytes 2097152
  49.5 0.0 copy-done.1
  49.5 0.0 copy-start
  49.5 0.7 %copy.12 = bf16[1,2,64,512]{3,2,1,0:T(8,128)(2,1)} copy(bf16[1,2,64,512]{3,2,1,0:T(8,128)(2,1)S(1)} %copy-done.1) | data formatting | bytes 262144
  50.2 0.3 copy-done
  50.5 0.7 %copy.13 = bf16[1,2,64,512]{3,2,1,0:T(8,128)(2,1)} copy(bf16[1,2,64,512]{3,2,1,0:T(8,128)(2,1)S(1)} %copy-done) | data formatting | bytes 262144
Async XLA Ops:
  47.2 2.3 %copy-start.1 = (bf16[1,2,64,512]{3,2,1,0:T(8,128)(2,1)S(1)}, bf16[1,2,64,512]{3,2,1,0:T(8,128)(2,1)}, u32[]{:S(2)}) copy-start(bf16[1,2,64,512]{3,2,1,0:T(8,128)(2,1)} %get-tuple-element.7) | copy-start | bytes 393220
  49.5 1.0 %copy-start = (bf16[1,2,64,512]{3,2,1,0:T(8,128)(2,1)S(1)}, bf16[1,2,64,512]{3,2,1,0:T(8,128)(2,1)}, u32[]{:S(2)}) copy-start(bf16[1,2,64,512]{3,2,1,0:T(8,128)(2,1)} %get-tuple-element.8) | copy-start | bytes 393220

commit v4 on v2

--- a/solution.py
+++ b/solution.py
@@ -32,8 +32,7 @@
     q_buf,
     do_buf,
     dq_buf,
-    k_win,
-    v_win,
+    win,
     part_out,
     part_in,
     own_sum,
@@ -69,18 +68,20 @@
         return (block >= 0) & (block < 2 * shards)
 
     length_load = pltpu.make_async_copy(lengths_hbm, lengths, length_sem.at[0])
+    own_loads = []
     loads = []
     for half in range(2):
         for stage in range(stages):
             at = pl.ds(stage * stage_width, stage_width)
-            for which, (mine, win) in enumerate(((keys, k_win), (values, v_win))):
-                loads.append(
+            for which, mine in enumerate((keys, values)):
+                own_loads.append(
                     pltpu.make_async_copy(
                         mine.at[0, half, :, at],
-                        win.at[half, stage, REACH],
+                        win.at[half, stage, REACH, which],
                         own_sem.at[half, which, stage],
                     )
                 )
+    for half in range(2):
         loads += [
             pltpu.make_async_copy(query.at[0, half], q_buf.at[half], load_sem.at[half, 0]),
             pltpu.make_async_copy(grad_out.at[0, half], do_buf.at[half], load_sem.at[half, 1]),
@@ -98,8 +99,10 @@
             pl.semaphore_signal(barrier, inc=1, device_id=place(me + d))
 
     length_load.start()
-    for copy in loads:
+    for copy in own_loads + loads:
         copy.start()
+    for copy in own_loads:
+        copy.wait()
     pl.semaphore_wait(barrier, jnp.minimum(me, 2) + jnp.minimum(shards - 1 - me, 2))
 
     def send(present, src, dst, block, send_sem, recv_sem):
@@ -146,100 +149,81 @@
     def kv_lanes(stage):
         return pl.ds(pl.multiple_of(stage * stage_width, stage_width), stage_width)
 
-    def kv_send_args(half, d, stage):
-        at = kv_lanes(stage)
-        for which, (mine, win) in enumerate(((keys, k_win), (values, v_win))):
-            if d < REACH:
-                block, present = blocks[half] + d, exists(blocks[half] + d)
-                src = mine.at[0, half, :, at]
-            else:
-                block = blocks[half] + 1
-                present = exists(block) & exists(blocks[half] - 2)
-                src = win.at[half, stage, REACH - 2]
-
-            def dst(target_half, win=win):
-                return win.at[target_half, stage, REACH - d]
-
-            def recv(target_half, which=which):
-                return kv_recv.at[target_half, d - 1, which, stage]
-
-            yield present, src, dst, block, kv_send.at[half, d - 1, which, stage], recv
-
-    def start_kv(half, d, stage):
-        for args in kv_send_args(half, d, stage):
-            send(*args)
-
-    def finish_kv(half, d, stage):
-        for args in kv_send_args(half, d, stage):
-            await_send(*args)
+    def kv_args(half, d, stage):
+        present = exists(blocks[half] + min(d, 2))
+        if d == REACH:
+            present = exists(blocks[half] + 1) & exists(blocks[half] - 2)
+        return (
+            present,
+            win.at[half, stage, REACH if d < REACH else REACH - 2],
+            lambda target_half: win.at[target_half, stage, REACH - d],
+            blocks[half] + (1 if d == REACH else d),
+            kv_send.at[half, d - 1, stage],
+            lambda target_half: kv_recv.at[target_half, d - 1, stage],
+        )
 
     def await_kv(half, d, stage):
-        for which, win in enumerate((k_win, v_win)):
-            await_recv(
-                exists(blocks[half] - d),
-                win.at[half, stage, REACH - d],
-                kv_send.at[half, d - 1, which, stage],
-                kv_recv.at[half, d - 1, which, stage],
-            )
+        await_recv(
+            exists(blocks[half] - d),
+            win.at[half, stage, REACH - d],
+            kv_send.at[half, d - 1, stage],
+            kv_recv.at[half, d - 1, stage],
+        )
 
     def relay_kv(stage):
         for half in range(2):
             await_kv(half, 2, stage)
-            start_kv(half, 3, stage)
+            send(*kv_args(half, 3, stage))
+
+    part_slots = {1: pl.ds(0, 2), 2: pl.ds(2, 1)}
+    slot_of = {1: 0, 3: 1, 2: 2}
 
     def part_args(half, d, stage):
+        at = part_slots[d]
         return (
             exists(blocks[half] - d),
-            part_out.at[half, stage, d - 1],
-            lambda target_half: part_in.at[target_half, stage, d - 1],
-            blocks[half] - (1 if d == REACH else d),
+            part_out.at[half, stage, at],
+            lambda target_half: part_in.at[target_half, stage, at],
+            blocks[half] - d,
             part_send.at[half, d - 1, stage],
             lambda target_half: part_recv.at[target_half, d - 1, stage],
         )
 
-    def finish_part(half, d, stage):
-        await_send(*part_args(half, d, stage))
-
     def await_part(half, d, stage):
-        if d == REACH:
-            present = exists(blocks[half] + 1) & exists(blocks[half] - 2)
-        else:
-            present = exists(blocks[half] + d)
         await_recv(
-            present,
-            part_in.at[half, stage, d - 1],
+            exists(blocks[half] + d),
+            part_in.at[half, stage, part_slots[d]],
             part_send.at[half, d - 1, stage],
             part_recv.at[half, d - 1, stage],
         )
 
     def relay_part(stage):
         for half in range(2):
-            await_part(half, 3, stage)
-            part_out[half, stage, 1] = (
-                part_out[half, stage, 1].astype(jnp.float32)
-                + part_in[half, stage, 2].astype(jnp.float32)
+            await_part(half, 1, stage)
+            part_out[half, stage, 2] = (
+                part_out[half, stage, 2].astype(jnp.float32)
+                + part_in[half, stage, 1].astype(jnp.float32)
             ).astype(jnp.bfloat16)
             send(*part_args(half, 2, stage))
 
     for stage in range(stages):
         for d in (2, 1):
             for half in range(2):
-                start_kv(half, d, stage)
+                send(*kv_args(half, d, stage))
 
     for d in range(1, REACH + 1):
 
         @pl.when(me < d)
         def _():
             for stage in range(stages):
-                k_win[0, stage, REACH - d] = jnp.zeros((half_rows, stage_width), k_win.dtype)
-                v_win[0, stage, REACH - d] = jnp.zeros((half_rows, stage_width), v_win.dtype)
-
-    for half, d, missing in ((0, 3, me < 2), (1, 3, me < 1), (1, 2, me < 2), (1, 1, me < 1)):
+                win[0, stage, REACH - d] = jnp.zeros((2, half_rows, stage_width), win.dtype)
+
+    for slot, missing in ((0, me < 1), (1, me < 1), (2, me < 2)):
 
         @pl.when(missing)
         def _():
             for stage in range(stages):
-                part_in[half, stage, d - 1] = jnp.zeros(
+                part_in[1, stage, slot] = jnp.zeros(
                     (half_rows, 2 * stage_width), part_in.dtype
                 )
 
@@ -279,8 +263,8 @@
 
         q = rows_of(q_buf)
         do = rows_of(do_buf)
-        k = k_win[half, stage, :, :, key_at].reshape(window, HEAD)
-        v = v_win[half, stage, :, :, key_at].reshape(window, HEAD)
+        k = win[half, stage, :, 0, :, key_at].reshape(window, HEAD)
+        v = win[half, stage, :, 1, :, key_at].reshape(window, HEAD)
         rows = group_size * half_rows
         hidden = jnp.concatenate([bias[half]] * (rows // LANES), 1)
         scores = lax.dot_general(k, q, NT, preferred_element_type=jnp.float32)
@@ -303,7 +287,7 @@
         for at, term in ((key_at, dk), (value_at, dv)):
             for d in range(1, REACH + 1):
                 top_row = (REACH - d) * half_rows
-                part_out[half, stage, d - 1, :, at] = term[top_row : top_row + half_rows].astype(
+                part_out[half, stage, slot_of[d], :, at] = term[top_row : top_row + half_rows].astype(
                     jnp.bfloat16
                 )
             own_sum[half, stage, :, at] = term[far:]
@@ -331,9 +315,8 @@
             return inner
 
         lax.fori_loop(0, 2 * stage_heads, unit_step, 0)
-        for d in (3, 1):
-            for half in range(2):
-                send(*part_args(half, d, stage))
+        for half in range(2):
+            send(*part_args(half, 1, stage))
         return carried
 
     lax.fori_loop(0, stages, stage_step, 0)
@@ -345,11 +328,10 @@
     relay_part(stages - 1)
     for stage in range(stages):
         for half in range(2):
-            for d in (1, 2):
-                await_part(half, d, stage)
+            await_part(half, 2, stage)
             total = own_sum[half, stage]
-            for d in (1, 2):
-                total = total + part_in[half, stage, d - 1].astype(jnp.float32)
+            for slot in (0, 2):
+                total = total + part_in[half, stage, slot].astype(jnp.float32)
             total = total.astype(jnp.bfloat16)
             grad_keys[0, half, :, kv_lanes(stage)] = total[:, :stage_width]
             grad_values[0, half, :, kv_lanes(stage)] = total[:, stage_width:]
@@ -359,8 +341,9 @@
     for stage in range(stages):
         for half in range(2):
             for d in range(1, REACH + 1):
-                finish_kv(half, d, stage)
-                finish_part(half, d, stage)
+                await_send(*kv_args(half, d, stage))
+                if d < REACH:
+                    await_send(*part_args(half, d, stage))
 
 
 def on_device(query, keys, values, grad_out, lengths):
@@ -391,8 +374,7 @@
             pltpu.VMEM(wide_half, bf16),
             pltpu.VMEM(wide_half, bf16),
             pltpu.VMEM(wide_half, bf16),
-            pltpu.VMEM((2, STAGES, REACH + 1, half_rows, kv_width // STAGES), bf16),
-            pltpu.VMEM((2, STAGES, REACH + 1, half_rows, kv_width // STAGES), bf16),
+            pltpu.VMEM((2, STAGES, REACH + 1, 2, half_rows, kv_width // STAGES), bf16),
             pltpu.VMEM((2, STAGES, REACH, half_rows, 2 * kv_width // STAGES), bf16),
             pltpu.VMEM((2, STAGES, REACH, half_rows, 2 * kv_width // STAGES), bf16),
             pltpu.VMEM((2, STAGES, half_rows, 2 * kv_width // STAGES), f32),
@@ -401,10 +383,10 @@
             dma((2, 2)),
             dma((2, 2, STAGES)),
             dma((2,)),
-            dma((2, REACH, 2, STAGES)),
-            dma((2, REACH, 2, STAGES)),
             dma((2, REACH, STAGES)),
             dma((2, REACH, STAGES)),
+            dma((2, 2, STAGES)),
+            dma((2, 2, STAGES)),
         ],
         compiler_params=pltpu.CompilerParams(
             collective_id=0, has_side_effects=True, vmem_limit_bytes=60 * 1024 * 1024

time: 45.3 us -> 46.3 us (1.022)
  the two profiles are of different devices: /device:TPU:1 before, /device:TPU:6 now
where the time goes in v4:
time: 46.3 us; the launch traced here: 46.2 us
  Pallas kernels  41.6 us (90%)
  local copies, waits for them, and re-layouts  3.93 us (8%)
  between operations  0.65 us (1%)
    pallas_call x1, Pallas kernels, on_device(): pl.pallas_call(functools.partial(kernel, shards, lax.axis_size('ctx'), si...  41.6 us
    unnamed x7, local copies, waits for them, and re-layouts  3.93 us

profile of v4, /device:TPU:6, one launch (start us, length us, event | category | flops | bytes accessed | tf_op | source)
XLA Modules:
  0.0 46.2 jit_solution(988471367599470267)
XLA Ops:
  0.6 41.6 %shard_map.76 = (bf16[1,2,64,4096]{3,2,1,0:T(8,128)(2,1)}, bf16[1,2,64,512]{3,2,1,0:T(8,128)(2,1)}, bf16[1,2,64,512]{3,2,1,0:T(8,128)(2,1)}) custom-call(s32[32]{0:T(128)} %lengths_hbm.1, bf16[1,2,64,4096]{3,2,1,0:T(8,128)(2,1)} %query.1, bf16[1,2,64,512]{3,2,1,0:T(8,128)(2,1)} %keys.1, bf16[1,2,64,512]{3,2,1,0:T(8,128)(2,1)} %values.1, ...), custom_call_target="tpu_custom_call" | custom-call | flops 1342177280 | bytes 4194304 | tf_op jit(solution)/shard_map/pallas_call | solution.py:363
  42.2 0.0 copy-start.1
  42.2 2.3 %copy.11 = bf16[1,2,64,4096]{3,2,1,0:T(8,128)(2,1)} copy(bf16[1,2,64,4096]{3,2,1,0:T(8,128)(2,1)} %get-tuple-element.6) | data formatting | bytes 2097152
  44.5 0.0 copy-done.1
  44.6 0.0 copy-start
  44.6 0.7 %copy.12 = bf16[1,2,64,512]{3,2,1,0:T(8,128)(2,1)} copy(bf16[1,2,64,512]{3,2,1,0:T(8,128)(2,1)S(1)} %copy-done.1) | data formatting | bytes 262144
  45.2 0.3 copy-done
  45.5 0.7 %copy.13 = bf16[1,2,64,512]{3,2,1,0:T(8,128)(2,1)} copy(bf16[1,2,64,512]{3,2,1,0:T(8,128)(2,1)S(1)} %copy-done) | data formatting | bytes 262144
Async XLA Ops:
  42.2 2.3 %copy-start.1 = (bf16[1,2,64,512]{3,2,1,0:T(8,128)(2,1)S(1)}, bf16[1,2,64,512]{3,2,1,0:T(8,128)(2,1)}, u32[]{:S(2)}) copy-start(bf16[1,2,64,512]{3,2,1,0:T(8,128)(2,1)} %get-tuple-element.7) | copy-start | bytes 393220
  44.6 1.0 %copy-start = (bf16[1,2,64,512]{3,2,1,0:T(8,128)(2,1)S(1)}, bf16[1,2,64,512]{3,2,1,0:T(8,128)(2,1)}, u32[]{:S(2)}) copy-start(bf16[1,2,64,512]{3,2,1,0:T(8,128)(2,1)} %get-tuple-element.8) | copy-start | bytes 393220

commit v5 on v4

--- a/solution.py
+++ b/solution.py
@@ -11,6 +11,7 @@
 HEAD = 128
 REACH = 3
 STAGES = 2
+PIECES = 2
 LANES = 128
 NT = (((1,), (1,)), ((), ()))
 NN = (((1,), (0,)), ((), ()))
@@ -304,11 +305,11 @@
         def unit_step(u, inner):
             unit(lax.rem(u, 2), stage, lax.div(u, 2))
 
-            @pl.when((u == 0) & (stage + 1 < stages))
+            @pl.when((u == 1) & (stage + 1 < stages))
             def _():
                 relay_kv(stage + 1)
 
-            @pl.when((u == 1) & (stage > 0))
+            @pl.when((u == 2 * stage_heads - 1) & (stage > 0))
             def _():
                 relay_part(stage - 1)
 
@@ -344,6 +345,27 @@
                 await_send(*kv_args(half, d, stage))
                 if d < REACH:
                     await_send(*part_args(half, d, stage))
+
+
+def hand_on(*refs):
+    count = len(refs) // 2
+    sems = refs[-1]
+    copies = []
+    for i in range(count):
+        src, dst = refs[i], refs[count + i]
+        rows = src.shape[2] // PIECES
+        for half in range(2):
+            for piece in range(PIECES):
+                at = pl.ds(piece * rows, rows)
+                copies.append(
+                    pltpu.make_async_copy(
+                        src.at[0, half, at], dst.at[0, half, at], sems.at[i, half, piece]
+                    )
+                )
+    for copy in copies:
+        copy.start()
+    for copy in copies:
+        copy.wait()
 
 
 def on_device(query, keys, values, grad_out, lengths):
@@ -360,7 +382,7 @@
     in_hbm = pl.BlockSpec(memory_space=pltpu.HBM)
     vmem = pl.BlockSpec(memory_space=pltpu.VMEM)
     wide_half = (2, half_rows, query.shape[3])
-    return pl.pallas_call(
+    grads = pl.pallas_call(
         functools.partial(kernel, shards, lax.axis_size("ctx"), sizes),
         out_shape=(
             jax.ShapeDtypeStruct(query.shape, bf16),
@@ -395,6 +417,14 @@
             flops=20 * half_rows * window * query.shape[3], bytes_accessed=4 << 20, transcendentals=0
         ),
     )(lengths, query, keys, values, grad_out)
+    return pl.pallas_call(
+        hand_on,
+        out_shape=tuple(jax.ShapeDtypeStruct(grad.shape, bf16) for grad in grads),
+        in_specs=[anywhere] * 3,
+        out_specs=(anywhere,) * 3,
+        scratch_shapes=[dma((3, 2, PIECES))],
+        compiler_params=pltpu.CompilerParams(vmem_limit_bytes=60 * 1024 * 1024),
+    )(*grads)
 
 
 def solution(mesh):

time: 46.3 us -> 84.7 us (1.83)
  Pallas kernels: 41.6 us -> 83.9 us
  local copies, waits for them, and re-layouts: 3.93 us -> 0 us
    pallas_call x0 -> x1, Pallas kernels: none -> 40.9 us  [on_device(): pl.pallas_call(hand_on, out_shape=tuple((jax.ShapeDtypeStruct(grad.shape,...]
    unnamed x7 -> x0, local copies, waits for them, and re-layouts: 3.93 us -> none
    pallas_call x1, Pallas kernels: 41.6 us -> 43 us  [on_device(): pl.pallas_call(functools.partial(kernel, shards, lax.axis_size('ctx'), si...]
where the time goes in v5:
time: 84.7 us; the launch traced here: 84.6 us
  Pallas kernels  83.9 us (99%)
    pallas_call x1, Pallas kernels, on_device(): pl.pallas_call(functools.partial(kernel, shards, lax.axis_size('ctx'), si...  43 us
    pallas_call x1, Pallas kernels, on_device(): pl.pallas_call(hand_on, out_shape=tuple((jax.ShapeDtypeStruct(grad.shape,...  40.9 us

profile of v5, /device:TPU:6, one launch (start us, length us, event | category | flops | bytes accessed | tf_op | source)
XLA Modules:
  0.0 84.6 jit_solution(7624630722227745056)
XLA Ops:
  0.6 43.0 %shard_map.76 = (bf16[1,2,64,4096]{3,2,1,0:T(8,128)(2,1)}, bf16[1,2,64,512]{3,2,1,0:T(8,128)(2,1)}, bf16[1,2,64,512]{3,2,1,0:T(8,128)(2,1)}) custom-call(s32[32]{0:T(128)} %lengths_hbm.1, bf16[1,2,64,4096]{3,2,1,0:T(8,128)(2,1)} %query.1, bf16[1,2,64,512]{3,2,1,0:T(8,128)(2,1)} %keys.1, bf16[1,2,64,512]{3,2,1,0:T(8,128)(2,1)} %values.1, ...), custom_call_target="tpu_custom_call" | custom-call | flops 1342177280 | bytes 4194304 | tf_op jit(solution)/shard_map/pallas_call | solution.py:385
  43.6 40.9 %shard_map.77 = (bf16[1,2,64,4096]{3,2,1,0:T(8,128)(2,1)}, bf16[1,2,64,512]{3,2,1,0:T(8,128)(2,1)}, bf16[1,2,64,512]{3,2,1,0:T(8,128)(2,1)}) custom-call(bf16[1,2,64,4096]{3,2,1,0:T(8,128)(2,1)} %get-tuple-element.6.refs_0_, bf16[1,2,64,512]{3,2,1,0:T(8,128)(2,1)} %get-tuple-element.7.refs_1_, bf16[1,2,64,512]{3,2,1,0:T(8,128)(2,1)} %get-tuple-element.8.refs_2_), custom_call_target="tpu_custom_call" | custom-call | tf_op jit(solution)/shard_map/pallas_call | solution.py:420

commit v6 on v4

--- a/solution.py
+++ b/solution.py
@@ -10,7 +10,7 @@
 
 HEAD = 128
 REACH = 3
-STAGES = 2
+STAGES = 1
 LANES = 128
 NT = (((1,), (1,)), ((), ()))
 NN = (((1,), (0,)), ((), ()))
@@ -296,35 +296,24 @@
     for copy in loads:
         copy.wait()
 
-    def stage_step(stage, carried):
+    stores = []
+    for stage in range(stages):
         for half in range(2):
             for d in (1, 3):
                 await_kv(half, d, stage)
-
-        def unit_step(u, inner):
-            unit(lax.rem(u, 2), stage, lax.div(u, 2))
-
-            @pl.when((u == 0) & (stage + 1 < stages))
-            def _():
-                relay_kv(stage + 1)
-
-            @pl.when((u == 1) & (stage > 0))
-            def _():
-                relay_part(stage - 1)
-
-            return inner
-
-        lax.fori_loop(0, 2 * stage_heads, unit_step, 0)
-        for half in range(2):
+            lax.fori_loop(
+                0, stage_heads, lambda head, c: (unit(half, stage, head), c)[1], 0
+            )
             send(*part_args(half, 1, stage))
-        return carried
-
-    lax.fori_loop(0, stages, stage_step, 0)
-    stores = []
-    for half in range(2):
-        store = pltpu.make_async_copy(dq_buf.at[half], grad_query.at[0, half], store_sem.at[half])
-        store.start()
-        stores.append(store)
+            if stage == stages - 1:
+                store = pltpu.make_async_copy(
+                    dq_buf.at[half], grad_query.at[0, half], store_sem.at[half]
+                )
+                store.start()
+                stores.append(store)
+        if stage + 1 < stages:
+            relay_kv(stage + 1)
+            relay_part(stage)
     relay_part(stages - 1)
     for stage in range(stages):
         for half in range(2):
@@ -344,6 +333,29 @@
                 await_send(*kv_args(half, d, stage))
                 if d < REACH:
                     await_send(*part_args(half, d, stage))
+
+
+def hand_on(*refs):
+    count = (len(refs) - 2) // 3
+    sources, results, held = refs[:count], refs[count : 2 * count], refs[2 * count : 3 * count]
+    into, out = refs[-2:]
+    pairs = []
+    for i in range(count):
+        for half in range(2):
+            here = held[i].at[half]
+            pairs.append(
+                (
+                    pltpu.make_async_copy(sources[i].at[0, half], here, into.at[i, half]),
+                    pltpu.make_async_copy(here, results[i].at[0, half], out.at[i, half]),
+                )
+            )
+    for load, _ in pairs:
+        load.start()
+    for load, store in pairs:
+        load.wait()
+        store.start()
+    for _, store in pairs:
+        store.wait()
 
 
 def on_device(query, keys, values, grad_out, lengths):
@@ -360,7 +372,7 @@
     in_hbm = pl.BlockSpec(memory_space=pltpu.HBM)
     vmem = pl.BlockSpec(memory_space=pltpu.VMEM)
     wide_half = (2, half_rows, query.shape[3])
-    return pl.pallas_call(
+    grads = pl.pallas_call(
         functools.partial(kernel, shards, lax.axis_size("ctx"), sizes),
         out_shape=(
             jax.ShapeDtypeStruct(query.shape, bf16),
@@ -395,6 +407,15 @@
             flops=20 * half_rows * window * query.shape[3], bytes_accessed=4 << 20, transcendentals=0
         ),
     )(lengths, query, keys, values, grad_out)
+    return pl.pallas_call(
+        hand_on,
+        out_shape=tuple(jax.ShapeDtypeStruct(grad.shape, bf16) for grad in grads),
+        in_specs=[anywhere] * 3,
+        out_specs=(anywhere,) * 3,
+        scratch_shapes=[pltpu.VMEM(grad.shape[1:], bf16) for grad in grads]
+        + [dma((3, 2)), dma((3, 2))],
+        compiler_params=pltpu.CompilerParams(vmem_limit_bytes=60 * 1024 * 1024),
+    )(*grads)
 
 
 def solution(mesh):

time: 46.3 us -> 44.5 us (0.961)
  the two profiles are of different devices: /device:TPU:6 before, /device:TPU:10 now
where the time goes in v6:
time: 44.5 us; the launch traced here: 44.3 us
  Pallas kernels  43.7 us (98%)
  between operations  0.64 us (1%)
    pallas_call x1, Pallas kernels, on_device(): pl.pallas_call(functools.partial(kernel, shards, lax.axis_size('ctx'), si...  41.5 us
    pallas_call x1, Pallas kernels, on_device(): pl.pallas_call(hand_on, out_shape=tuple((jax.ShapeDtypeStruct(grad.shape,...  2.19 us

profile of v6, /device:TPU:10, one launch (start us, length us, event | category | flops | bytes accessed | tf_op | source)
XLA Modules:
  0.0 44.3 jit_solution(7339630398087617447)
XLA Ops:
  0.6 41.5 %shard_map.76 = (bf16[1,2,64,4096]{3,2,1,0:T(8,128)(2,1)}, bf16[1,2,64,512]{3,2,1,0:T(8,128)(2,1)}, bf16[1,2,64,512]{3,2,1,0:T(8,128)(2,1)}) custom-call(s32[32]{0:T(128)} %lengths_hbm.1, bf16[1,2,64,4096]{3,2,1,0:T(8,128)(2,1)} %query.1, bf16[1,2,64,512]{3,2,1,0:T(8,128)(2,1)} %keys.1, bf16[1,2,64,512]{3,2,1,0:T(8,128)(2,1)} %values.1, ...), custom_call_target="tpu_custom_call" | custom-call | flops 1342177280 | bytes 4194304 | tf_op jit(solution)/shard_map/pallas_call | solution.py:375
  42.1 2.2 %shard_map.77 = (bf16[1,2,64,4096]{3,2,1,0:T(8,128)(2,1)}, bf16[1,2,64,512]{3,2,1,0:T(8,128)(2,1)}, bf16[1,2,64,512]{3,2,1,0:T(8,128)(2,1)}) custom-call(bf16[1,2,64,4096]{3,2,1,0:T(8,128)(2,1)} %get-tuple-element.6.refs_0_, bf16[1,2,64,512]{3,2,1,0:T(8,128)(2,1)} %get-tuple-element.7.refs_1_, bf16[1,2,64,512]{3,2,1,0:T(8,128)(2,1)} %get-tuple-element.8.refs_2_), custom_call_target="tpu_custom_call" | custom-call | tf_op jit(solution)/shard_map/pallas_call | solution.py:410

commit v7 on v6

--- a/solution.py
+++ b/solution.py
@@ -301,9 +301,14 @@
         for half in range(2):
             for d in (1, 3):
                 await_kv(half, d, stage)
-            lax.fori_loop(
-                0, stage_heads, lambda head, c: (unit(half, stage, head), c)[1], 0
-            )
+            pair = 2 if stage_heads % 2 == 0 else 1
+
+            def heads_step(step, carried):
+                for at in range(pair):
+                    unit(half, stage, step * pair + at)
+                return carried
+
+            lax.fori_loop(0, stage_heads // pair, heads_step, 0)
             send(*part_args(half, 1, stage))
             if stage == stages - 1:
                 store = pltpu.make_async_copy(

time: 44.5 us -> 44 us (0.989)
  Pallas kernels: 43.7 us -> 43.2 us
    pallas_call x1, Pallas kernels: 41.5 us -> 41 us  [on_device(): pl.pallas_call(functools.partial(kernel, shards, lax.axis_size('ctx'), si...]
where the time goes in v7:
time: 44 us; the launch traced here: 43.8 us
  Pallas kernels  43.2 us (98%)
  between operations  0.64 us (1%)
    pallas_call x1, Pallas kernels, on_device(): pl.pallas_call(functools.partial(kernel, shards, lax.axis_size('ctx'), si...  41 us
    pallas_call x1, Pallas kernels, on_device(): pl.pallas_call(hand_on, out_shape=tuple((jax.ShapeDtypeStruct(grad.shape,...  2.19 us

profile of v7, /device:TPU:10, one launch (start us, length us, event | category | flops | bytes accessed | tf_op | source)
XLA Modules:
  0.0 43.8 jit_solution(11401378758157779414)
XLA Ops:
  0.6 41.0 %shard_map.76 = (bf16[1,2,64,4096]{3,2,1,0:T(8,128)(2,1)}, bf16[1,2,64,512]{3,2,1,0:T(8,128)(2,1)}, bf16[1,2,64,512]{3,2,1,0:T(8,128)(2,1)}) custom-call(s32[32]{0:T(128)} %lengths_hbm.1, bf16[1,2,64,4096]{3,2,1,0:T(8,128)(2,1)} %query.1, bf16[1,2,64,512]{3,2,1,0:T(8,128)(2,1)} %keys.1, bf16[1,2,64,512]{3,2,1,0:T(8,128)(2,1)} %values.1, ...), custom_call_target="tpu_custom_call" | custom-call | flops 1342177280 | bytes 4194304 | tf_op jit(solution)/shard_map/pallas_call | solution.py:380
  41.6 2.2 %shard_map.77 = (bf16[1,2,64,4096]{3,2,1,0:T(8,128)(2,1)}, bf16[1,2,64,512]{3,2,1,0:T(8,128)(2,1)}, bf16[1,2,64,512]{3,2,1,0:T(8,128)(2,1)}) custom-call(bf16[1,2,64,4096]{3,2,1,0:T(8,128)(2,1)} %get-tuple-element.6.refs_0_, bf16[1,2,64,512]{3,2,1,0:T(8,128)(2,1)} %get-tuple-element.7.refs_1_, bf16[1,2,64,512]{3,2,1,0:T(8,128)(2,1)} %get-tuple-element.8.refs_2_), custom_call_target="tpu_custom_call" | custom-call | tf_op jit(solution)/shard_map/pallas_call | solution.py:415
